TPU v7x, 32 devices: a whole 2x2x4 slice. The times are simulated.
32 devices in a mesh: rows: 8 (over y, x, core), seq: 4 (over z).
Axes of the slice: x: 2, y: 2, z: 4, core: 2. Of those that a mesh axis runs over, the one named last changes fastest.
Arguments:
- canvas: bfloat16 [8, 2048, 512], P('rows', 'seq'), may hold values from -6 to 6
- memory: bfloat16 [8, 512, 512], P('rows', 'seq'), may hold values from -6 to 6
- cotangent: bfloat16 [8, 2048, 512], P('rows', 'seq'), may hold values from -6 to 6
- canvas_lengths: int32 [8], P('rows'), may hold values from 1844 to 2048, as said below
- canvas_segments: int32 [8, 2048], P('rows', 'seq'), may hold values from 0 to 3, as said below
- memory_segments: int32 [8, 512], P('rows', 'seq'), may hold values from 0 to 3, as said below
- memory_lengths: int32 [8], P('rows'), may hold values from 448 to 512, as said below
- self_query: bfloat16 [512, 512], replicated, may hold values from -0.25 to 0.25
- self_key: bfloat16 [512, 512], replicated, may hold values from -0.25 to 0.25
- self_value: bfloat16 [512, 512], replicated, may hold values from -0.25 to 0.25
- self_output: bfloat16 [512, 512], replicated, may hold values from -1.5 to 1.5
- self_query_bias: bfloat16 [512], replicated, may hold values from -2 to 2
- self_value_bias: bfloat16 [512], replicated, may hold values from -2 to 2
- self_output_bias: bfloat16 [512], replicated, may hold values from -2 to 2
- first_gain: bfloat16 [512], replicated, may hold values from 0.25 to 1.75
- first_bias: bfloat16 [512], replicated, may hold values from -2 to 2
- cross_query: bfloat16 [512, 512], replicated, may hold values from -0.25 to 0.25
- cross_key: bfloat16 [512, 512], replicated, may hold values from -0.25 to 0.25
- cross_value: bfloat16 [512, 512], replicated, may hold values from -0.25 to 0.25
- cross_output: bfloat16 [512, 512], replicated, may hold values from -1 to 1
- cross_query_bias: bfloat16 [512], replicated, may hold values from -2 to 2
- cross_value_bias: bfloat16 [512], replicated, may hold values from -2 to 2
- cross_output_bias: bfloat16 [512], replicated, may hold values from -2 to 2
- second_gain: bfloat16 [512], replicated, may hold values from 0.25 to 1.75
- second_bias: bfloat16 [512], replicated, may hold values from -2 to 2
- expand_weight: bfloat16 [512, 2048], replicated, may hold values from -0.25 to 0.25
- expand_bias: bfloat16 [2048], replicated, may hold values from -2 to 2
- reduce_weight: bfloat16 [2048, 512], replicated, may hold values from -0.125 to 0.125
- reduce_bias: bfloat16 [512], replicated, may hold values from -2 to 2
- third_gain: bfloat16 [512], replicated, may hold values from 0.25 to 1.75
- third_bias: bfloat16 [512], replicated, may hold values from -2 to 2
- slot_weight: bfloat16 [1024, 512], replicated, may hold values from -0.1875 to 0.1875
- slot_bias: bfloat16 [512], replicated, may hold values from -2 to 2
Outputs:
- slot_states: bfloat16 [8, 2048, 512], P('rows', 'seq')
- canvas_grad: float32 [8, 2048, 512], P('rows', 'seq')
- memory_grad: float32 [8, 512, 512], P('rows', 'seq')
- grad_self_query: float32 [512, 512], replicated
- grad_self_key: float32 [512, 512], replicated
- grad_self_value: float32 [512, 512], replicated
- grad_self_output: float32 [512, 512], replicated
- grad_self_query_bias: float32 [512], replicated
- grad_self_value_bias: float32 [512], replicated
- grad_self_output_bias: float32 [512], replicated
- grad_first_gain: float32 [512], replicated
- grad_first_bias: float32 [512], replicated
- grad_cross_query: float32 [512, 512], replicated
- grad_cross_key: float32 [512, 512], replicated
- grad_cross_value: float32 [512, 512], replicated
- grad_cross_output: float32 [512, 512], replicated
- grad_cross_query_bias: float32 [512], replicated
- grad_cross_value_bias: float32 [512], replicated
- grad_cross_output_bias: float32 [512], replicated
- grad_second_gain: float32 [512], replicated
- grad_second_bias: float32 [512], replicated
- grad_expand_weight: float32 [512, 2048], replicated
- grad_expand_bias: float32 [2048], replicated
- grad_reduce_weight: float32 [2048, 512], replicated
- grad_reduce_bias: float32 [512], replicated
- grad_third_gain: float32 [512], replicated
- grad_third_bias: float32 [512], replicated
- grad_slot_weight: float32 [1024, 512], replicated
- grad_slot_bias: float32 [512], replicated
Inputs may be any that keep to these rules, and one draw needn't show every extreme that they name: `canvas_lengths`: some row is full; every canvas has live positions. `canvas_segments`: never falls along a row; each of the 4 canvases holds 256 to 1024 positions, one exactly 1024. `memory_segments`: never falls along a row; canvas k begins within 32 positions of k * 128. `memory_lengths`: some row is full; every canvas has live memory positions.
All inputs are finite; a program needn't handle non-finite values.
Results may differ from a plain program's by a relative error of at most 0.024.
Values may be sent and summed in bfloat16 or wider, within the bound.
No kernel may reach another device: no remote copies, remote signals or barrier semaphores. Data moves between devices by JAX's collectives and lax.ppermute only.
A program may use at most 192 MiB of HBM per device.

v0:
```python
import functools

import jax
import jax.numpy as jnp
from jax import lax
from jax.experimental import pallas as pl
from jax.experimental.pallas import tpu as pltpu
from jax.sharding import PartitionSpec as P

H = 8
HD = 64
PAIRS = H // 2
TILE = 256
TAIL = 16
LAST_SPLIT = 2
LATER_SPLIT = 0
TURNS = "EM1SMSEMSESMEMSSESMceSMsm"
VROWS = 80
ROOM = 58 * 1024 * 1024

masked_score = -30000.0
epsilon = 1e-05
gelu_scale = 0.7978845608028654
gelu_cubic = 0.044715
safe_square = 3600.0
bf16 = jnp.bfloat16
f32 = jnp.float32


def cost(microseconds):
    return pl.CostEstimate(flops=int(microseconds * 1.1e9), bytes_accessed=0, transcendentals=0)


def matmul(left, right):
    return jnp.dot(left, right, preferred_element_type=f32)


def times_transposed(left, right):
    return lax.dot_general(left, right, (((1,), (1,)), ((), ())), preferred_element_type=f32)


def bfloat(values):
    return values.astype(bf16)


def widen(values):
    return values.astype(f32)


def head_rows(dtype):
    row = lax.broadcasted_iota(jnp.int32, (16, H * HD), 0)
    column = lax.broadcasted_iota(jnp.int32, (16, H * HD), 1)
    return jnp.where(column // HD == row, 1.0, 0.0).astype(dtype)


def one_head(pair_columns, side):
    lane = lax.broadcasted_iota(jnp.int32, pair_columns.shape, 1)
    wanted = lane < HD if side == 0 else lane >= HD
    return jnp.where(wanted, widen(pair_columns), 0.0).astype(bf16)


def neighbours(place):
    inner = jnp.logical_or(place == 1, place == 2)
    beside = place + 1 - 2 * lax.rem(place, 2)
    across = 3 - place
    far = jnp.where(inner, across + 1 - 2 * lax.rem(across, 2), 3 - beside)
    return inner, beside, across, far


def window_moves(place, blocks, window, tails, semaphores):
    own, side, middle, middle_far, side_far = blocks
    inner, beside, across, far = neighbours(place)
    outer = jnp.logical_not(inner)
    T = window.shape[1]

    def move(block, slot, index):
        return (
            pltpu.make_async_copy(block.at[pl.ds(0, T)], window.at[slot], semaphores.at[2 * index]),
            pltpu.make_async_copy(
                block.at[pl.ds(T, TAIL)], tails.at[slot], semaphores.at[2 * index + 1]
            ),
        )

    def near(act):
        for copy in move(own, place, 0) + move(side, beside, 1):
            act(copy)

        @pl.when(inner)
        def _():
            for copy in move(middle, across, 2):
                act(copy)

    def distant(act):
        @pl.when(inner)
        def _():
            for copy in move(middle_far, far, 3):
                act(copy)

        @pl.when(outer)
        def _():
            for copy in move(side_far, far, 3):
                act(copy)

    return near, distant


def is_outer(place):
    return jnp.logical_or(place == 0, place == 3)


def present_tiles(place, per, with_far):
    reach = 2 if with_far else 1
    return jnp.maximum(place - reach, 0) * per, jnp.minimum(place + reach + 1, 4) * per


def masked_chances(lse):
    return jnp.exp(masked_score - lse)


def masked_terms(lse, upstream):
    chances = jnp.concatenate([masked_chances(lse), jnp.zeros((8, lse.shape[1]), f32)], axis=0)
    terms = matmul(bfloat(chances), upstream)
    return jnp.sum(jnp.where(head_rows(f32) > 0.0, terms, 0.0), axis=0, keepdims=True)


def start(copy):
    copy.start()


def wait(copy):
    copy.wait()


def no_codes(codes, keycodes, pivot):
    T = codes.shape[1]
    for slot in range(4):
        codes[slot : slot + 1, :] = jnp.full((1, T), 1.0, f32) * jnp.where(slot < pivot, -8.0, 8.0)
        keycodes[slot : slot + 1, :] = jnp.full((1, T), -9.0, f32)


def read_codes(codes, keycodes, tails, slot, length):
    T = codes.shape[1]
    lane = lax.broadcasted_iota(jnp.int32, (1, T), 1)
    code = widen(tails[slot, 0:1, 0:T])
    codes[pl.ds(slot, 1), :] = code
    keycodes[pl.ds(slot, 1), :] = jnp.where(slot * T + lane < length, code, -1.0)


def near_codes(codes, keycodes, tails, place, length):
    inner, beside, across, _ = neighbours(place)
    read_codes(codes, keycodes, tails, place, length)
    read_codes(codes, keycodes, tails, beside, length)

    @pl.when(inner)
    def _():
        read_codes(codes, keycodes, tails, across, length)


def tile_range(codes, first_code, last_code):
    below = jnp.sum(jnp.where(codes[...] < first_code, 1, 0))
    through = jnp.sum(jnp.where(codes[...] <= last_code, 1, 0))
    return below // TILE, (through + TILE - 1) // TILE


def as_column(row):
    return jnp.transpose(jnp.broadcast_to(row, (128, row.shape[1])))


def column_codes(keycodes, columns, tile, T):
    per = T // TILE
    row = keycodes[pl.ds(tile // per, 1), pl.ds(pl.multiple_of(lax.rem(tile, per) * TILE, TILE), TILE)]
    columns[pl.ds(pl.multiple_of(tile * TILE, TILE), TILE), :] = as_column(row)


def tile_rows(window, tile):
    per = window.shape[1] // TILE
    return window[tile // per, pl.ds(pl.multiple_of(lax.rem(tile, per) * TILE, TILE), TILE), :]


def split_heads(rows, sides):
    for head in range(H):
        sides[head] = one_head(rows[:, 128 * (head // 2) : 128 * (head // 2) + 128], head % 2)


def visible_in(columns, at, code_row):
    column = columns[at, :]
    return jnp.concatenate([column] * (code_row.shape[1] // 128), axis=1) == code_row


def look_at(at, keys, q_sides, columns, code_row, summit):
    visible = visible_in(columns, at, code_row)
    for head in range(H):
        scores = times_transposed(keys[head // 2, at, :], q_sides[head])
        scores = jnp.where(visible, scores, masked_score)
        summit[head : head + 1, :] = jnp.maximum(
            summit[head : head + 1, :], jnp.max(scores, axis=0, keepdims=True)
        )


def blend_at(at, keys, values_t, q_sides, columns, code_row, summit, total):
    visible = visible_in(columns, at, code_row)
    for head in range(H):
        scores = jnp.where(visible, times_transposed(keys[head // 2, at, :], q_sides[head]), masked_score)
        powers = bfloat(jnp.exp(scores - summit[head : head + 1, :]))
        total[head] += matmul(values_t[head, :, at], powers)


def normalise(total, summit, lse, blend_t):
    for head in range(H):
        mass = total[head, HD : HD + 1, :]
        blend_t[HD * head : HD * head + HD, :] = total[head, 0:HD, :] / mass
        lse[head : head + 1, :] = summit[head : head + 1, :] + jnp.log(mass)
    return bfloat(jnp.transpose(blend_t[...]))


def row_corrections(upstream, blended):
    products = widen(upstream) * widen(blended)
    coarse = bfloat(products)
    fine = bfloat(products - widen(coarse))
    ones_of_heads = head_rows(bf16)
    both = times_transposed(ones_of_heads, coarse) + times_transposed(ones_of_heads, fine)
    return both[0:H]


def step_back(at, keys, keys_t, values, q_sides, u_sides, columns, code_row, lse, fixes, query_t, grad_keys, grad_values):
    visible = visible_in(columns, at, code_row)
    for pair in range(PAIRS):
        k = keys[pair, at, :]
        v = values[pair, at, :]
        key_add = value_add = None
        for head in (2 * pair, 2 * pair + 1):
            q_side, u_side = q_sides[head], u_sides[head]
            scores = jnp.where(visible, times_transposed(k, q_side), masked_score)
            chances = jnp.exp(scores - lse[head : head + 1, :])
            chance_grad = times_transposed(v, u_side) - fixes[head : head + 1, :]
            score_grad = bfloat(jnp.where(visible, chances * chance_grad, 0.0))
            to_values = matmul(bfloat(chances), u_side)
            to_keys = matmul(score_grad, q_side)
            value_add = to_values if value_add is None else value_add + to_values
            key_add = to_keys if key_add is None else key_add + to_keys
            rows = slice(HD * head, HD * head + HD)
            query_t[rows, :] += matmul(keys_t[rows, at], score_grad)
        grad_keys[pair, at, :] = key_add
        grad_values[pair, at, :] = value_add


def tile_at(tile):
    return pl.ds(pl.multiple_of(tile * TILE, TILE), TILE)


def project_forward(tile, window, keycodes, columns, keys, values_t, wk, weights_t, bias_t):
    x = tile_rows(window, tile)
    at = tile_at(tile)
    k = bfloat(matmul(x, wk[...]))
    for pair in range(PAIRS):
        keys[pair, at, :] = k[:, 128 * pair : 128 * pair + 128]
    v_t = bfloat(times_transposed(weights_t, x) + bias_t)
    for head in range(H):
        values_t[head, 0:HD, at] = v_t[HD * head : HD * head + HD]
        values_t[head, HD:VROWS, at] = jnp.ones((VROWS - HD, TILE), bf16)
    column_codes(keycodes, columns, tile, window.shape[1])
    return times_transposed(head_rows(bf16), k * k)


def self_near_kernel(
    ready, done, numbers, own, side, middle, segments, vectors, wv, wq, wk,
    queries, total, reach_out,
    window, tails, codes, keycodes, columns, keys, values_t, zeros, q_sides, semaphores,
):
    T, D = queries.shape
    place, length = numbers[0], numbers[1]
    near, _ = window_moves(place, (own, side, middle, middle, side), window, tails, semaphores)
    near(start)
    no_codes(codes, keycodes, place)
    ready()
    weights_t = jnp.transpose(wv[...])
    bias_t = as_column(vectors[BV1 : BV1 + 1, :])[:, 0:1]
    near(wait)
    near_codes(codes, keycodes, tails, place, length)
    low, high = tile_range(codes, numbers[4].astype(f32), numbers[5].astype(f32))
    rows_q = bfloat((matmul(window[place], wq[...]) + vectors[BQ1 : BQ1 + 1, :]) * 0.125)
    queries[...] = rows_q
    done(0)
    split_heads(rows_q, q_sides)

    def project(tile, reach):
        return jnp.maximum(
            reach, project_forward(tile, window, keycodes, columns, keys, values_t, wk, weights_t, bias_t)
        )

    key_reach = lax.fori_loop(low, high, project, jnp.zeros((16, TILE), f32))
    reach_out[...] = jnp.broadcast_to(jnp.max(key_reach, axis=1, keepdims=True), (16, 128))
    zeros[...] = jnp.zeros_like(zeros)
    total[...] = jnp.zeros_like(total)
    code_row = segments[...].astype(f32)

    def blend(tile, _):
        blend_at(tile_at(tile), keys, values_t, q_sides, columns, code_row, zeros, total)
        return 0

    lax.fori_loop(low, high, blend, 0)


def self_far_kernel(
    ready, done, numbers, own, side, middle, middle_far, side_far,
    wk, wv, segments, vectors, queries, near_reach, opposite, near_total,
    out, lse,
    window, tails, codes, keycodes, columns, keys, values_t, summit, total, blend_t, q_sides, semaphores,
):
    T, D = out.shape
    place, length = numbers[0], numbers[1]
    _, _, _, far = neighbours(place)
    near, distant = window_moves(
        place, (own, side, middle, middle_far, side_far), window, tails, semaphores
    )
    distant(start)
    no_codes(codes, keycodes, far)
    ready()
    weights_t = jnp.transpose(wv[...])
    bias_t = as_column(vectors[BV1 : BV1 + 1, :])[:, 0:1]
    ones_of_heads = head_rows(bf16)
    rows_q = queries[...]
    split_heads(rows_q, q_sides)
    query_reach = jnp.max(times_transposed(ones_of_heads, rows_q * rows_q), axis=1, keepdims=True)
    first, last = numbers[4].astype(f32), numbers[5].astype(f32)
    distant(wait)
    read_codes(codes, keycodes, tails, far, length)
    low, high = tile_range(codes, first, last)

    def project(tile, reach):
        return jnp.maximum(
            reach, project_forward(tile, window, keycodes, columns, keys, values_t, wk, weights_t, bias_t)
        )

    key_reach = lax.fori_loop(low, high, project, jnp.zeros((16, TILE), f32))
    key_reach = jnp.maximum(jnp.max(key_reach, axis=1, keepdims=True), near_reach[:, 0:1])
    wide = jnp.max(query_reach * key_reach) > safe_square
    summit[...] = jnp.zeros_like(summit)
    total[...] = near_total[...]
    code_row = segments[...].astype(f32)

    per = T // TILE
    low_here, high_here = present_tiles(place, per, True)

    @pl.when(wide)
    def _():
        near(start)
        near(wait)
        near_codes(codes, keycodes, tails, place, length)
        lax.fori_loop(low_here, high_here, project, jnp.zeros((16, TILE), f32))
        total[...] = jnp.zeros_like(total)
        summit[...] = jnp.full(summit.shape, masked_score, f32)

        def look(tile, _):
            look_at(tile_at(tile), keys, q_sides, columns, code_row, summit)
            return 0

        lax.fori_loop(low_here, high_here, look, 0)

        @pl.when(is_outer(place))
        def _():
            sums = times_transposed(weights_t, opposite[...])
            column = sums[:, 2:3] + sums[:, 3:4] + T * bias_t
            for head in range(H):
                part = jnp.concatenate(
                    [column[HD * head : HD * head + HD], jnp.full((VROWS - HD, 1), T, f32)], axis=0
                )
                total[head] = part * jnp.exp(masked_score - summit[head : head + 1, :])

    def blend(tile, _):
        blend_at(tile_at(tile), keys, values_t, q_sides, columns, code_row, summit, total)
        return 0

    lax.fori_loop(
        jnp.where(wide, low_here, low), jnp.where(wide, high_here, high), blend, 0
    )
    out[...] = normalise(total, summit, lse, blend_t)


def project_backward(tile, window, keycodes, columns, keys, keys_t, values, wk, wv, bias, weights_t):
    x = tile_rows(window, tile)
    at = tile_at(tile)
    k = bfloat(matmul(x, wk[...]))
    v = bfloat(matmul(x, wv[...]) + bias)
    for pair in range(PAIRS):
        keys[pair, at, :] = k[:, 128 * pair : 128 * pair + 128]
        values[pair, at, :] = v[:, 128 * pair : 128 * pair + 128]
    keys_t[:, at] = bfloat(times_transposed(weights_t, x))
    column_codes(keycodes, columns, tile, window.shape[1])


def tile_grads(at, grad_keys, grad_values):
    gk = jnp.concatenate([bfloat(grad_keys[pair, at, :]) for pair in range(PAIRS)], axis=1)
    gv = jnp.concatenate([bfloat(grad_values[pair, at, :]) for pair in range(PAIRS)], axis=1)
    return gk, gv


def back_far_kernel(
    ready, done, numbers, middle_far, side_far,
    segments, vectors, wk, wv, queries, upstream, blended, lse, opposite,
    part_out, grad_k, grad_v, value_sum, query_t,
    window, tails, codes, keycodes, columns, keys, keys_t, values, grad_keys, grad_values,
    q_sides, u_sides, fixes, semaphores,
):
    T, D = queries.shape
    place, length = numbers[0], numbers[1]
    _, _, _, far = neighbours(place)
    _, distant = window_moves(
        place, (side_far, side_far, side_far, middle_far, side_far), window, tails, semaphores
    )
    distant(start)
    ready()
    no_codes(codes, keycodes, far)
    part_out[...] = jnp.zeros_like(part_out)
    query_t[...] = jnp.zeros_like(query_t)
    grad_k[...] = jnp.zeros_like(grad_k)
    grad_v[...] = jnp.zeros_like(grad_v)
    value_sum[...] = jnp.zeros_like(value_sum)
    distant(wait)
    read_codes(codes, keycodes, tails, far, length)
    low, high = tile_range(codes, numbers[4].astype(f32), numbers[5].astype(f32))
    code_row = segments[...].astype(f32)
    per = T // TILE
    deep = jnp.max(masked_chances(lse[...])) > 0.0
    low = jnp.where(deep, far * per, low)
    high = jnp.where(deep, far * per + per, high)

    @pl.when(jnp.logical_and(deep, is_outer(place)))
    def _():
        terms = masked_terms(lse[...], upstream[...])
        terms_8 = jnp.broadcast_to(terms, (TAIL, D))
        row = lax.broadcasted_iota(jnp.int32, (TAIL, D), 0)
        rows = jnp.where(jnp.logical_or(row == 2, row == 3), widen(opposite[...]), 0.0)
        grad_v[...] += matmul(jnp.transpose(rows), jnp.where(row < 4, terms_8, 0.0))
        value_sum[0:1, :] += T * terms

    @pl.when(high > low)
    def _():
        weights_t = jnp.transpose(wk[...])
        split_heads(queries[...], q_sides)
        split_heads(upstream[...], u_sides)
        fixes[...] = row_corrections(upstream[...], blended[...])

        def step(tile, _):
            project_backward(
                tile, window, keycodes, columns, keys, keys_t, values, wk, wv,
                vectors[BV1 : BV1 + 1, :], weights_t,
            )
            at = tile_at(tile)
            step_back(
                at, keys, keys_t, values, q_sides, u_sides, columns, code_row, lse, fixes, query_t,
                grad_keys, grad_values,
            )
            gk, gv = tile_grads(at, grad_keys, grad_values)
            x_t = jnp.transpose(tile_rows(window, tile))
            grad_k[...] += matmul(x_t, gk)
            grad_v[...] += matmul(x_t, gv)
            value_sum[0:1, :] += summed(gv)
            inside = pl.ds(pl.multiple_of(lax.rem(tile, T // TILE) * TILE, TILE), TILE)
            part_out[inside, :] = bfloat(times_transposed(gk, wk[...]) + times_transposed(gv, wv[...]))
            return 0

        lax.fori_loop(low, high, step, 0)


def back_near_kernel(
    ready, done, numbers, own, side, middle,
    segments, vectors, wk, wv, queries, upstream, blended, lse, far_query_t,
    wq, entering, far_k, far_v, far_sum, sums_one, sums_two,
    canvas_out, middle_out, side_out, sent, kept,
    window, tails, codes, keycodes, columns, keys, keys_t, values, grad_keys, grad_values,
    q_sides, u_sides, fixes, query_t, grad_k, grad_v, semaphores,
):
    T, D = queries.shape
    place, length = numbers[0], numbers[1]
    per = T // TILE
    near, _ = window_moves(place, (own, side, middle, middle, side), window, tails, semaphores)
    near(start)
    no_codes(codes, keycodes, place)
    ready(9)
    weights_t = jnp.transpose(wk[...])
    split_heads(queries[...], q_sides)
    split_heads(upstream[...], u_sides)
    fixes[...] = row_corrections(upstream[...], blended[...])
    query_t[...] = far_query_t[...]
    middle_out[...] = jnp.zeros_like(middle_out)
    side_out[...] = jnp.zeros_like(side_out)
    near(wait)
    near_codes(codes, keycodes, tails, place, length)
    low, high = tile_range(codes, numbers[4].astype(f32), numbers[5].astype(f32))
    code_row = segments[...].astype(f32)
    deep = jnp.max(masked_chances(lse[...])) > 0.0
    low_here, high_here = present_tiles(place, per, False)
    low, high = jnp.where(deep, low_here, low), jnp.where(deep, high_here, high)

    def step(tile, _):
        project_backward(
            tile, window, keycodes, columns, keys, keys_t, values, wk, wv,
            vectors[BV1 : BV1 + 1, :], weights_t,
        )
        step_back(
            tile_at(tile), keys, keys_t, values, q_sides, u_sides, columns, code_row, lse, fixes, query_t,
            grad_keys, grad_values,
        )
        return 0

    lax.fori_loop(low, high, step, 0)
    ready()
    grad_k[...] = far_k[...]
    grad_v[...] = far_v[...]
    query_rows = bfloat(jnp.transpose(query_t[...])) * 0.125
    canvas_out[...] = entering[...] + times_transposed(query_rows, wq[...])
    half = kept.shape[0]
    half_side = numbers[3]
    put_block(bfloat(matmul(jnp.transpose(window[place]), query_rows)), 0, half, half_side, sent, kept)
    inner, beside, across, _ = neighbours(place)

    def fold(tile, value_sum):
        block = tile // per
        inside = pl.ds(pl.multiple_of(lax.rem(tile, per) * TILE, TILE), TILE)
        gk, gv = tile_grads(tile_at(tile), grad_keys, grad_values)
        x_t = jnp.transpose(tile_rows(window, tile))
        grad_k[...] += matmul(x_t, gk)
        grad_v[...] += matmul(x_t, gv)
        part = times_transposed(gk, wk[...]) + times_transposed(gv, wv[...])

        @pl.when(block == place)
        def _():
            canvas_out[inside, :] += part

        @pl.when(jnp.logical_and(inner, block == across))
        def _():
            middle_out[inside, :] = bfloat(part)

        @pl.when(block == beside)
        def _():
            side_out[inside, :] = bfloat(part)

        return value_sum + summed(gv)

    value_sum = lax.fori_loop(low, high, fold, far_sum[0:1, :])
    done(0, 1, 2)
    put_block(bfloat(grad_k[...]), D, half, half_side, sent, kept)
    put_block(bfloat(grad_v[...]), 2 * D, half, half_side, sent, kept)
    vector_sums = jnp.concatenate(
        [sums_one[...], sums_two[...], summed(query_rows), value_sum, jnp.zeros((6, D), f32)], axis=0
    )
    put_block(bfloat(vector_sums), 3 * D, half, half_side, sent, kept)
    spare = 2 * half - 3 * D - 32
    put_block(jnp.zeros((spare, D), bf16), 3 * D + 32, half, half_side, sent, kept)


VMEM_BLOCK = pl.BlockSpec(memory_space=pltpu.VMEM)
SMEM_BLOCK = pl.BlockSpec(memory_space=pltpu.SMEM)
ANY_BLOCK = pl.BlockSpec(memory_space=pl.ANY)
HBM_BLOCK = pl.BlockSpec(memory_space=pltpu.HBM)


class Numbers:
    def __init__(self, numbers, length, memory_length, segments):
        T = segments.shape[1]
        self.refs = [
            (numbers, (0,)), (length, (0,)), (memory_length, (0,)), (numbers, (1,)),
            (segments, (0, 0)), (segments, (0, T - 1)),
        ]

    def __getitem__(self, index):
        ref, at = self.refs[index]
        return ref[at]


def run_kernel(kernel, name, microseconds, out_shapes, small, far, near, scratch, ties=(), out_far=0):
    kept = out_shapes[: len(out_shapes) - out_far]
    counts = [len(small), len(far), len(near), len(ties), len(kept), out_far, len(scratch), len(near), len(kept), 1]

    def body(*refs):
        parts, at = [], 0
        for count in counts:
            parts.append(refs[at : at + count])
            at += count
        small_refs, far_refs, held, _, outs, own_outs, scratch_refs, copies, results, (semaphores,) = parts
        loads = [
            pltpu.make_async_copy(a, b, semaphores.at[n]) for n, (a, b) in enumerate(zip(held, copies))
        ]
        leaving = {
            n: pltpu.make_async_copy(a, b, semaphores.at[len(loads) + n])
            for n, (a, b) in enumerate(zip(results, outs))
        }
        left = []
        for load in loads:
            load.start()
        waiting = list(loads)

        def ready(count=len(loads)):
            for load in waiting[:count]:
                load.wait()
            del waiting[:count]

        def done(*numbers):
            for n in numbers:
                copy = leaving.pop(n)
                copy.start()
                left.append(copy)

        kernel(ready, done, Numbers(*small_refs), *far_refs, *copies, *results, *own_outs, *scratch_refs)
        ready()
        done(*list(leaving))
        for copy in left:
            copy.wait()

    return pl.pallas_call(
        body,
        out_shape=[jax.ShapeDtypeStruct(shape, kind) for shape, kind in out_shapes],
        in_specs=[SMEM_BLOCK] * len(small)
        + [HBM_BLOCK] * (len(far) + len(near))
        + [ANY_BLOCK] * len(ties),
        out_specs=[HBM_BLOCK] * len(out_shapes),
        scratch_shapes=[
            *scratch,
            *[pltpu.VMEM(w.shape, w.dtype) for w in near],
            *[pltpu.VMEM(shape, kind) for shape, kind in kept],
            pltpu.SemaphoreType.DMA((len(near) + len(kept),)),
        ],
        compiler_params=pltpu.CompilerParams(vmem_limit_bytes=ROOM),
        cost_estimate=cost(microseconds),
        name=name,
    )(*small, *far, *near, *ties)


def window_scratch(T, D):
    return [
        pltpu.VMEM((4, T, D), bf16),
        pltpu.VMEM((4, TAIL, D), bf16),
        pltpu.VMEM((4, T), f32),
        pltpu.VMEM((4, T), f32),
        pltpu.VMEM((4 * T, 128), f32),
    ]


def self_near(numbers, segments, blocks, weights, vectors, ties=()):
    T, D = segments.shape[1], vectors.shape[1]
    wq, wk, wv = weights
    return run_kernel(
        self_near_kernel, "self_near", 13,
        [((T, D), bf16), ((H, VROWS, T), f32), ((16, 128), f32)],
        numbers, blocks[:3], [segments, vectors, wv, wq, wk],
        window_scratch(T, D)
        + [
            pltpu.VMEM((PAIRS, 4 * T, 128), bf16),
            pltpu.VMEM((H, VROWS, 4 * T), bf16),
            pltpu.VMEM((H, T), f32),
            pltpu.VMEM((H, T, 128), bf16),
            pltpu.SemaphoreType.DMA((8,)),
        ],
        ties,
    )


def self_far(numbers, segments, blocks, weights, vectors, queries, total, reach, opposite, ties=()):
    T, D = queries.shape
    return run_kernel(
        self_far_kernel, "self_far", 7,
        [((T, D), bf16), ((H, T), f32)],
        numbers, blocks, [*weights[1:], segments, vectors, queries, reach, opposite, total],
        window_scratch(T, D)
        + [
            pltpu.VMEM((PAIRS, 4 * T, 128), bf16),
            pltpu.VMEM((H, VROWS, 4 * T), bf16),
            pltpu.VMEM((H, T), f32),
            pltpu.VMEM((H, VROWS, T), f32),
            pltpu.VMEM((D, T), f32),
            pltpu.VMEM((H, T, 128), bf16),
            pltpu.SemaphoreType.DMA((8,)),
        ],
        ties,
    )


def backward_scratch(T, D):
    return window_scratch(T, D) + [
        pltpu.VMEM((PAIRS, 4 * T, 128), bf16),
        pltpu.VMEM((D, 4 * T), bf16),
        pltpu.VMEM((PAIRS, 4 * T, 128), bf16),
        pltpu.VMEM((PAIRS, 4 * T, 128), f32),
        pltpu.VMEM((PAIRS, 4 * T, 128), f32),
        pltpu.VMEM((H, T, 128), bf16),
        pltpu.VMEM((H, T, 128), bf16),
        pltpu.VMEM((H, T), f32),
    ]


def back_far(numbers, segments, blocks, weights, vectors, queries, blended, upstream, lse, opposite, ties=()):
    T, D = queries.shape
    return run_kernel(
        back_far_kernel, "back_far", 8,
        [((T, D), bf16), ((D, D), f32), ((D, D), f32), ((8, D), f32), ((D, T), f32)],
        numbers, blocks[3:],
        [segments, vectors, *weights[1:], queries, upstream, blended, lse, opposite],
        backward_scratch(T, D) + [pltpu.SemaphoreType.DMA((8,))],
        ties,
    )


def back_near(numbers, segments, blocks, weights, vectors, queries, blended, upstream, lse, entering, sums, far, ties=()):
    T, D = queries.shape
    wq, wk, wv = weights
    far_k, far_v, far_sum, far_query_t = far
    rows = 3 * D // 2 + D // 4
    return run_kernel(
        back_near_kernel, "back_near", 22,
        [((T, D), f32), ((T, D), bf16), ((T, D), bf16), ((rows, D), bf16), ((rows, D), bf16)],
        numbers, blocks[:3],
        [
            segments, vectors, wk, wv, queries, upstream, blended, lse, far_query_t,
            wq, entering, far_k, far_v, far_sum, *sums,
        ],
        backward_scratch(T, D)
        + [
            pltpu.VMEM((D, T), f32),
            pltpu.VMEM((D, D), f32),
            pltpu.VMEM((D, D), f32),
            pltpu.SemaphoreType.DMA((8,)),
        ],
        ties,
    )


def pack_kernel(ready, done, numbers, canvas, cotangent, *refs):
    *small, wide, segments, memory_segments, memory, vectors, payload, last, extras, held, semaphores = refs
    T, D = canvas.shape
    here = memory.shape[0]
    arrive = pltpu.make_async_copy(canvas, held, semaphores.at[0])
    arrive.start()
    rows = pltpu.make_async_copy(held, payload.at[pl.ds(0, T)], semaphores.at[3])
    copy = pltpu.make_async_copy(cotangent.at[pl.ds(T - TAIL, TAIL)], last, semaphores.at[1])
    copy.start()
    arrive.wait()
    rows.start()
    ready()

    def padded(row):
        if row.shape[1] == D:
            return row
        return jnp.concatenate([row, jnp.zeros((1, D - row.shape[1]), f32)], axis=1)

    row = lax.broadcasted_iota(jnp.int32, (TAIL, D), 0)
    copy.wait()
    codes = jnp.broadcast_to(padded(segments[...].astype(f32)), (TAIL, D))
    carried = jnp.broadcast_to(widen(last[...])[TAIL - 1 : TAIL], (TAIL, D))
    row_sum = jnp.broadcast_to(summed(held[...]), (TAIL, D))
    rest_of_sum = row_sum - widen(bfloat(row_sum))
    extras[0:TAIL, :] = bfloat(
        jnp.where(
            row == 0, codes,
            jnp.where(row == 1, carried, jnp.where(row == 2, row_sum, jnp.where(row == 3, rest_of_sum, 0.0))),
        )
    )
    extras[TAIL : TAIL + here, :] = memory[...]
    codes = jnp.broadcast_to(padded(memory_segments[...].astype(f32)), (TAIL, D))
    extras[TAIL + here : 2 * TAIL + here, :] = bfloat(jnp.where(row == 0, codes, 0.0))
    rest = pltpu.make_async_copy(extras, payload.at[pl.ds(T, 2 * TAIL + here)], semaphores.at[2])
    rest.start()
    for index, vector in enumerate(small):
        vectors[index : index + 1, :] = widen(vector[...])[None, :]
    values = widen(wide[...])
    for c in range(values.shape[0] // D):
        vectors[len(small) + c : len(small) + c + 1, :] = values[c * D : c * D + D][None, :]
    rows.wait()
    rest.wait()


def pack(numbers, small, wide, segments, memory_segments, memory, canvas, cotangent):
    T, D = canvas.shape
    size = 2 * TAIL + memory.shape[0]
    return run_kernel(
        pack_kernel, "pack", 2,
        [((len(small) + wide.shape[0] // D, D), f32), ((T + size, D), bf16)],
        numbers, [canvas, cotangent], [*small, wide, segments, memory_segments, memory],
        [pltpu.VMEM((TAIL, D), bf16), pltpu.VMEM((size, D), bf16), pltpu.VMEM((T, D), bf16), pltpu.SemaphoreType.DMA((4,))],
        (), 1,
    )


BQ1, BV1, BO1, G1, B1, BQ2, BV2, BO2, G2, B2, BR, G3, B3, BS, BE = range(15)


def smooth_gate(inputs):
    square = inputs * inputs
    bent = jnp.tanh(gelu_scale * inputs * (1.0 + gelu_cubic * square))
    half = 0.5 * (1.0 + bent)
    slope = half + 0.5 * inputs * (1.0 - bent * bent) * (
        gelu_scale * (1.0 + 3.0 * gelu_cubic * square)
    )
    return inputs * half, slope


def norm_forward(inputs):
    average = jnp.mean(inputs, axis=-1, keepdims=True)
    centred = inputs - average
    scaling = lax.rsqrt(jnp.mean(centred * centred, axis=-1, keepdims=True) + epsilon)
    return centred * scaling, scaling


def norm_backward(upstream, gain, normal, scaling):
    scaled = upstream * gain
    return scaling * (
        scaled
        - jnp.mean(scaled, axis=-1, keepdims=True)
        - normal * jnp.mean(scaled * normal, axis=-1, keepdims=True)
    )


def summed(values):
    return jnp.sum(widen(values), axis=0, keepdims=True)


def memory_moves(place, blocks, last_memory, gathered, semaphores, first):
    own, side, middle, middle_far, side_far = blocks
    size = gathered.shape[1]
    begin = own.shape[0] - size
    inner, beside, across, far = neighbours(place)

    def move(block, slot, index):
        return pltpu.make_async_copy(
            block.at[pl.ds(begin, size)], gathered.at[slot], semaphores.at[first + index]
        )

    def run(act):
        for copy in (move(own, place, 0), move(side, beside, 1)):
            act(copy)

        @pl.when(inner)
        def _():
            for copy in (move(middle, across, 2), move(middle_far, far, 3)):
                act(copy)

        @pl.when(jnp.logical_not(inner))
        def _():
            last = pltpu.make_async_copy(last_memory, gathered.at[3 - place], semaphores.at[first + 3])
            for copy in (move(side_far, far, 2), last):
                act(copy)

    return run


def memory_rows(gathered, memory, columns, memory_length):
    count, size, width = gathered.shape
    here = size - TAIL
    lane = lax.broadcasted_iota(jnp.int32, (1, here), 1)
    for b in range(count):
        span = slice(b * here, (b + 1) * here)
        memory[span, :] = gathered[b, 0:here, :]
        code = widen(gathered[b, here : here + 1, 0:here])
        columns[span, :] = as_column(jnp.where(b * here + lane < memory_length, code, -1.0))


def put_block(block, start, half, side, sent, kept):
    size = block.shape[0]
    for part in range(2):
        low, high = max(start, part * half), min(start + size, (part + 1) * half)
        if low >= high:
            continue
        rows = block[low - start : high - start]
        at = slice(low - part * half, high - part * half)

        @pl.when(side == part)
        def _():
            kept[at, :] = rows

        @pl.when(side != part)
        def _():
            sent[at, :] = rows


def forward_kernel(
    ready, done, numbers, own, side, middle, middle_far, side_far, last_memory,
    segments, vectors, ck, cv, canvas, blended, wo, cq, co, we, wr, ws, cotangent,
    slots_out, last_out, first_state, normal_out, scaling_out, low_out, query_out, fetched_out,
    lse, second_out, sums, gathered, sent, kept,
    tails, memory, columns, keys, values_t, summit, total,
    blend_t, q_sides, hidden, slope, second, low2, early, semaphores,
):
    T, D = canvas.shape
    M = memory.shape[0]
    FF = we.shape[1]
    place, length, memory_length = numbers[0], numbers[1], numbers[2]
    edges = [
        pltpu.make_async_copy(side.at[pl.ds(T, TAIL)], tails.at[0], semaphores.at[0]),
        pltpu.make_async_copy(middle.at[pl.ds(T, TAIL)], tails.at[1], semaphores.at[1]),
    ]
    bring = memory_moves(
        place, (own, side, middle, middle_far, side_far), last_memory, gathered, semaphores, 2
    )
    bring(start)
    for copy in edges:
        copy.start()
    leaving = []

    half = sent.shape[0]
    half_side = numbers[3]

    def leave(block, index):
        early[pl.ds(index * D, D), :] = block
        part, start_row = divmod(index * D, half)
        source = early.at[pl.ds(index * D, D)]
        rows = pl.ds(start_row, D)

        @pl.when(half_side == part)
        def _():
            pltpu.make_async_copy(source, kept.at[rows], semaphores.at[6 + index]).start()

        @pl.when(half_side != part)
        def _():
            pltpu.make_async_copy(source, sent.at[rows], semaphores.at[6 + index]).start()

        leaving.append(pltpu.make_async_copy(source, kept.at[rows], semaphores.at[6 + index]))

    def vector(index):
        return vectors[index : index + 1, :]

    sums[...] = jnp.zeros_like(sums)
    ready(2)
    code_row = segments[...].astype(f32)

    bring(wait)
    memory_rows(gathered, memory, columns, memory_length)
    done(11)
    ready(2)
    k = bfloat(matmul(memory[...], ck[...]))
    for pair in range(PAIRS):
        keys[pair] = k[:, 128 * pair : 128 * pair + 128]
    bias_t = as_column(vector(BV2))[:, 0:1]
    v_t = bfloat(times_transposed(jnp.transpose(cv[...]), memory[...]) + bias_t)
    for head in range(H):
        values_t[head, 0:HD, :] = v_t[HD * head : HD * head + HD]
        values_t[head, HD:VROWS, :] = jnp.ones((VROWS - HD, M), bf16)

    ready(3)
    first_in = widen(canvas[...]) + matmul(blended[...], wo[...]) + vector(BO1)
    normal, scaling = norm_forward(first_in)
    normal_out[...] = normal
    scaling_out[...] = jnp.broadcast_to(scaling, (T, 128))
    done(3, 4)
    first = normal * vector(G1) + vector(B1)
    low = bfloat(first)
    low_out[...] = low
    ready(1)
    query_out[...] = bfloat((matmul(low, cq[...]) + vector(BQ2)) * 0.125)
    done(5, 6)

    ones_of_heads = head_rows(bf16)
    q_all = query_out[...]
    reach = jnp.max(
        jnp.max(times_transposed(ones_of_heads, q_all * q_all), axis=1, keepdims=True)
        * jnp.max(times_transposed(ones_of_heads, k * k), axis=1, keepdims=True)
    )
    wide = reach > safe_square
    summit[...] = jnp.zeros_like(summit)
    total[...] = jnp.zeros_like(total)
    split_heads(q_all, q_sides)
    tiles = [slice(t, t + TILE) for t in range(0, M, TILE)]

    @pl.when(wide)
    def _():
        summit[...] = jnp.full(summit.shape, masked_score, f32)
        for at in tiles:
            look_at(at, keys, q_sides, columns, code_row, summit)

    for at in tiles:
        blend_at(at, keys, values_t, q_sides, columns, code_row, summit, total)
    fetched = normalise(total, summit, lse, blend_t)
    fetched_out[...] = fetched
    done(7, 8)

    ready(1)
    second_in = first + matmul(fetched, co[...]) + vector(BO2)
    normal2, scaling2 = norm_forward(second_in)
    second[...] = normal2 * vector(G2) + vector(B2)
    low2[...] = bfloat(second[...])
    ready(2)
    third_in = second[...] + vector(BR)
    for c in range(FF // D):
        lanes = slice(c * D, (c + 1) * D)
        before = matmul(low2[...], we[:, lanes]) + vector(BE + c)
        gate, bend = smooth_gate(before)
        gate = bfloat(gate)
        hidden[:, lanes] = gate
        slope[:, lanes] = bend
        third_in += matmul(gate, wr[lanes, :])
    normal3, scaling3 = norm_forward(third_in)
    states = bfloat(normal3 * vector(G3) + vector(B3))
    first_state[...] = states[0:TAIL]

    for copy in edges:
        copy.wait()
    ready()
    inner = jnp.logical_or(place == 1, place == 2)
    beside_tail, across_tail = widen(tails[0]), widen(tails[1])
    after_code = jnp.where(place == 1, across_tail[0:1, 0:1], beside_tail[0:1, 0:1])
    before_code = jnp.where(place == 2, across_tail[0:1, T - 1 : T], beside_tail[0:1, T - 1 : T])
    before_row = jnp.where(place == 2, across_tail[1:2, :], beside_tail[1:2, :])
    lane = lax.broadcasted_iota(jnp.int32, (8, T), 1)
    codes8 = jnp.broadcast_to(code_row, (8, T))
    live = jnp.where(place * T + lane < length, codes8, -1.0)
    next_code = jnp.where(lane == T - 1, after_code, pltpu.roll(live, T - 1, 1))
    valid8 = jnp.where(
        jnp.logical_and(next_code == codes8, place * T + lane + 1 < length), 1.0, 0.0
    )
    valid = as_column(valid8[0:1, :])[:, 0:1]
    last_valid = jnp.where(
        jnp.logical_and(before_code == code_row[:, 0:1], jnp.logical_and(place > 0, place * T < length)),
        1.0, 0.0,
    )
    row = lax.broadcasted_iota(jnp.int32, (T, D), 0)
    following = bfloat(jnp.where(row == T - 1, 0.0, pltpu.roll(widen(states), T - 1, 0)))
    raw = matmul(states, ws[0:D, :]) + vector(BS) + matmul(following, ws[D : 2 * D, :])
    slots_out[...] = bfloat(raw * valid)
    last_out[...] = jnp.concatenate(
        [raw[T - 1 : T], jnp.broadcast_to(valid[T - 1 : T], (1, D)), jnp.zeros((6, D), f32)], axis=0
    )
    done(0, 1, 2)
    masked = widen(cotangent[...]) * valid
    shifted = jnp.where(row == 0, before_row * last_valid, pltpu.roll(masked, 1, 0))
    masked_low, shifted_low = bfloat(masked), bfloat(shifted)
    upstream = times_transposed(masked_low, ws[0:D, :]) + widen(
        bfloat(times_transposed(shifted_low, ws[D : 2 * D, :]))
    )
    states_t = jnp.transpose(states)
    leave(bfloat(matmul(states_t, masked_low)), 0)
    leave(bfloat(matmul(states_t, shifted_low)), 1)
    sums[0:1, :] = summed(masked)

    third_grad = norm_backward(upstream, vector(G3), normal3, scaling3)
    sums[1:2, :] = summed(upstream * normal3)
    sums[2:3, :] = summed(upstream)
    third_low = bfloat(third_grad)
    sums[3:4, :] = summed(third_low)
    low2_t = jnp.transpose(low2[...])
    second_up = third_grad
    for c in range(FF // D):
        lanes = slice(c * D, (c + 1) * D)
        leave(bfloat(matmul(jnp.transpose(hidden[:, lanes]), third_low)), 2 + FF // D + c)
        hidden_grad = bfloat(times_transposed(third_low, wr[lanes, :]))
        before_grad = bfloat(widen(hidden_grad) * slope[:, lanes])
        leave(bfloat(matmul(low2_t, before_grad)), 2 + c)
        sums[4 + c : 5 + c, :] = summed(before_grad)
        second_up += times_transposed(before_grad, we[:, lanes])
    second_out[...] = norm_backward(second_up, vector(G2), normal2, scaling2)
    sums[8:9, :] = summed(second_up * normal2)
    sums[9:10, :] = summed(second_up)
    for copy in leaving:
        copy.wait()


def backward_kernel(
    ready, done, numbers,
    second_grad, co, segments, vectors, gathered, query, ck, cv, fetched, lse, cq, normal, scaling, wo, low,
    blended, first_state, wv, self_lse,
    first_grad_out, upstream_out, memory_out, sent, kept, sums,
    memory, columns, keys, keys_t, values, grad_keys, grad_values, query_t, upstream2, q_sides, u_sides, fixes,
):
    T, D = low.shape
    M = memory.shape[0]
    half_side = numbers[3]
    sums[...] = jnp.zeros_like(sums)
    ready(2)
    low_grad = bfloat(second_grad[...])
    upstream2[...] = bfloat(times_transposed(low_grad, co[...]))
    ready(4)
    code_row = segments[...].astype(f32)
    gain = vectors[G1 : G1 + 1, :]
    memory_rows(gathered, memory, columns, numbers[2])
    split_heads(query[...], q_sides)
    ready(2)
    k = bfloat(matmul(memory[...], ck[...]))
    v = bfloat(matmul(memory[...], cv[...]) + vectors[BV2 : BV2 + 1, :])
    for pair in range(PAIRS):
        keys[pair] = k[:, 128 * pair : 128 * pair + 128]
        values[pair] = v[:, 128 * pair : 128 * pair + 128]
    keys_t[...] = jnp.transpose(k)
    ready(2)
    fixes[...] = row_corrections(upstream2[...], fetched[...])
    split_heads(upstream2[...], u_sides)
    query_t[...] = jnp.zeros_like(query_t)
    for tile in range(M // TILE):
        step_back(
            slice(tile * TILE, (tile + 1) * TILE), keys, keys_t, values, q_sides, u_sides, columns,
            code_row, lse, fixes, query_t, grad_keys, grad_values,
        )
    query_rows = bfloat(jnp.transpose(query_t[...])) * 0.125
    ready()
    first_up = second_grad[...] + times_transposed(query_rows, cq[...])
    first_grad = norm_backward(first_up, gain, normal[...], scaling[:, 0:1])
    first_grad_out[...] = first_grad
    first_low = bfloat(first_grad)
    upstream_out[...] = bfloat(times_transposed(first_low, wo[...]))
    done(0, 1)
    gk, gv = tile_grads(slice(0, M), grad_keys, grad_values)
    part = bfloat(times_transposed(gk, ck[...]) + times_transposed(gv, cv[...]))
    count, size, _ = memory_out.shape
    here = size - TAIL
    place = numbers[0]
    tail = lax.broadcasted_iota(jnp.int32, (TAIL, D), 0)
    terms = jnp.broadcast_to(masked_terms(self_lse[...], upstream_out[...]), (TAIL, D))
    opposite_row = times_transposed(bfloat(terms), wv[...])
    for b in range(count):
        memory_out[b, 0:here, :] = part[b * here : (b + 1) * here]
        rows = jnp.where(jnp.logical_and(tail == 0, place == b + 1), widen(first_state[...]), 0.0)
        rows += jnp.where(
            jnp.logical_and(tail == 1, jnp.logical_and(is_outer(place), place == 3 - b)), opposite_row, 0.0
        )
        memory_out[b, here:size, :] = bfloat(rows)
    done(2)
    half = 5 * D // 2
    memory_t = jnp.transpose(memory[...])
    put_block(bfloat(matmul(jnp.transpose(low[...]), query_rows)), 0, half, half_side, sent, kept)
    put_block(bfloat(matmul(memory_t, gk)), D, half, half_side, sent, kept)
    put_block(bfloat(matmul(memory_t, gv)), 2 * D, half, half_side, sent, kept)
    put_block(bfloat(matmul(jnp.transpose(fetched[...]), low_grad)), 3 * D, half, half_side, sent, kept)
    put_block(bfloat(matmul(jnp.transpose(blended[...]), first_low)), 4 * D, half, half_side, sent, kept)
    sums[0:1, :] = summed(low_grad)
    sums[1:2, :] = summed(query_rows)
    sums[2:3, :] = summed(gv)
    sums[3:4, :] = summed(first_up * normal[...])
    sums[4:5, :] = summed(first_up)
    sums[5:6, :] = summed(first_low)


def middle_forward(numbers, segments, canvas, blended, cotangent, vectors, blocks, last_memory, weights, ties=()):
    T, D = canvas.shape
    wo, ck, cv, cq, co, we, wr, ws = weights
    FF = we.shape[1]
    here = last_memory.shape[0] - TAIL
    M = 4 * here
    rows = 2 * D + 2 * FF
    return run_kernel(
        forward_kernel, "middle_forward", 24,
        [
            ((T, D), bf16), ((8, D), f32), ((TAIL, D), bf16), ((T, D), f32), ((T, 128), f32), ((T, D), bf16),
            ((T, D), bf16), ((T, D), bf16), ((H, T), f32), ((T, D), f32),
            ((16, D), f32), ((4, here + TAIL, D), bf16), ((rows // 2, D), bf16), ((rows // 2, D), bf16),
        ],
        numbers, [*blocks, last_memory],
        [segments, vectors, ck, cv, canvas, blended, wo, cq, co, we, wr, ws, cotangent],
        [
            pltpu.VMEM((2, TAIL, D), bf16),
            pltpu.VMEM((M, D), bf16),
            pltpu.VMEM((M, 128), f32),
            pltpu.VMEM((PAIRS, M, 128), bf16),
            pltpu.VMEM((H, VROWS, M), bf16),
            pltpu.VMEM((H, T), f32),
            pltpu.VMEM((H, VROWS, T), f32),
            pltpu.VMEM((D, T), f32),
            pltpu.VMEM((H, T, 128), bf16),
            pltpu.VMEM((T, FF), bf16),
            pltpu.VMEM((T, FF), f32),
            pltpu.VMEM((T, D), f32),
            pltpu.VMEM((T, D), bf16),
            pltpu.VMEM((rows, D), bf16),
            pltpu.SemaphoreType.DMA((6 + rows // D,)),
        ],
        ties, 2,
    )


def middle_backward(numbers, segments, blended, gathered, vectors, saved, weights, ties=()):
    T, D = blended.shape
    M = gathered.shape[0] * (gathered.shape[1] - TAIL)
    rows = 5 * D // 2
    normal, scaling, low, query, fetched, lse, second_grad, first_state, self_lse = saved
    wo, cq, ck, cv, co, wv = weights
    return run_kernel(
        backward_kernel, "middle_backward", 16,
        [
            ((T, D), f32), ((T, D), bf16), (gathered.shape, bf16),
            ((rows, D), bf16), ((rows, D), bf16), ((8, D), f32),
        ],
        numbers, [],
        [
            second_grad, co, segments, vectors, gathered, query, ck, cv, fetched, lse,
            cq, normal, scaling, wo, low, blended, first_state, wv, self_lse,
        ],
        [
            pltpu.VMEM((M, D), bf16),
            pltpu.VMEM((M, 128), f32),
            pltpu.VMEM((PAIRS, M, 128), bf16),
            pltpu.VMEM((D, M), bf16),
            pltpu.VMEM((PAIRS, M, 128), bf16),
            pltpu.VMEM((PAIRS, M, 128), f32),
            pltpu.VMEM((PAIRS, M, 128), f32),
            pltpu.VMEM((D, T), f32),
            pltpu.VMEM((T, D), bf16),
            pltpu.VMEM((H, T, 128), bf16),
            pltpu.VMEM((H, T, 128), bf16),
            pltpu.VMEM((H, T), f32),
        ],
        ties,
    )


def pieces(start, count, half):
    found = []
    for part in range(2):
        low, high = max(start, part * half), min(start + count, (part + 1) * half)
        if low < high:
            found.append((part, low - part * half, low - start, high - low))
    return found


def unpack_kernel(layout, ready, done, numbers, mine, came, *outs):
    half, D = mine.shape
    half_side = numbers[3]
    ready()
    for number, (out, starts) in enumerate(zip(outs, layout)):
        count = out.shape[0]
        for column, start_row in enumerate(starts):
            lanes = slice(column * D, (column + 1) * D)
            for part, there, here, rows in pieces(start_row, count, half):
                step = min(rows, 512)
                for at in range(0, rows, step):
                    size = min(step, rows - at)
                    source = slice(there + at, there + at + size)
                    target = slice(here + at, here + at + size)

                    @pl.when(half_side == part)
                    def _():
                        out[target, lanes] = widen(mine[source, :])

                    @pl.when(half_side != part)
                    def _():
                        out[target, lanes] = widen(came[source, :])

        done(number)


def unpack(numbers, name, mine, came, layout, ties=()):
    D = mine.shape[1]
    return run_kernel(
        functools.partial(unpack_kernel, [starts for _, starts in layout]), name, 4,
        [((count, D * len(starts)), f32) for count, starts in layout],
        numbers, [], [mine, came], [], ties,
    )


def finish_kernel(
    ready, done, numbers, memory_stays, memory_came, last_slot, slots, bottom, base, onward, outward,
    memory_grad, slots_out, canvas_grad,
):
    T, D = slots.shape
    here = memory_grad.shape[0]
    ready(4)
    summed_rows = widen(memory_stays[...]) + widen(memory_came[...])
    memory_grad[...] = summed_rows[0:here]
    done(0)
    next_state = bfloat(summed_rows[here : here + TAIL])
    ready(1)
    last_row = (last_slot[0:1, :] + matmul(next_state, bottom[...])[0:1]) * last_slot[1:2, :]
    row = lax.broadcasted_iota(jnp.int32, (TAIL, D), 0)
    slots_out[0 : T - TAIL, :] = slots[0 : T - TAIL, :]
    slots_out[T - TAIL : T, :] = bfloat(
        jnp.where(row == TAIL - 1, last_row, widen(slots[T - TAIL : T, :]))
    )
    done(1)
    ready()
    canvas_grad[...] = base[...] + summed_rows[here + 1 : here + 2] + widen(onward[...]) + widen(outward[...])


def finish(numbers, memory_stays, memory_came, last_slot, slots, bottom, base, onward, outward, ties=()):
    T, D = slots.shape
    return run_kernel(
        finish_kernel, "finish", 3,
        [((memory_stays.shape[0] - TAIL, D), f32), ((T, D), bf16), ((T, D), f32)],
        numbers, [], [memory_stays, memory_came, last_slot, slots, bottom, base, onward, outward], [], ties,
    )


SIDE = [(0, 1), (1, 0), (2, 3), (3, 2)]
MIDDLE = [(1, 2), (2, 1)]
OUTWARD = [(1, 0), (2, 3)]
INWARD = [(0, 1), (3, 2)]


def routes():
    bits = [("rows", 1 << b) for b in range((lax.axis_size("rows") - 1).bit_length())]
    along = [("seq", 1 << b) for b in range((lax.axis_size("seq") - 1).bit_length())]
    return bits[0], bits[1:], bits[:0:-1], along


def swap(block, step):
    axis, bit = step
    return lax.ppermute(block, axis, [(i, i ^ bit) for i in range(lax.axis_size(axis))])


def side_of(step):
    axis, bit = step
    return jnp.where((lax.axis_index(axis) & bit) != 0, 1, 0)


def halves(terms, step):
    side = side_of(step)
    half = terms[0].shape[0] // 2

    def part(which):
        pieces = [widen(lax.dynamic_slice_in_dim(t, which * half, half)) for t in terms]
        return bfloat(sum(pieces[1:], pieces[0]))

    return part(1 - side), part(side)


def ordered(block, came, step):
    side = side_of(step) == 1
    return jnp.where(side, came, block), jnp.where(side, block, came)


class Order:
    def __init__(self):
        self.last = []

    def made(self, *values):
        self.last = list(values)

    def after(self, *values):
        if not self.last:
            return values
        values, _ = lax.optimization_barrier((values, tuple(self.last)))
        return values


class Summing:
    def __init__(self, order, sent, kept, split):
        self.order = order
        self.split = split
        self.steps = self.run(sent, kept)
        self.whole = None
        next(self.steps)

    def step(self):
        if self.whole is not None:
            return
        try:
            self.order.made(*next(self.steps))
        except StopIteration as end:
            self.whole = end.value

    def finish(self):
        while self.whole is None:
            self.step()
        return self.whole

    def take(self, blocks):
        return self.order.after(*blocks)

    def run(self, sent, kept):
        first, up, down, along = routes()
        came = swap(sent, first)
        yield [sent]
        (came,) = self.take([came])
        size = kept.shape[0]
        if self.split == 2:
            ways = [(up, 0, size // 2), (down, size // 2, size // 2)]
        else:
            ways = [(down if self.split else up, 0, size)]
        lanes = [[kept[at : at + n], came[at : at + n]] for _, at, n in ways]
        for number in range(len(up)):
            parts = [halves(terms, way[number]) for terms, (way, _, _) in zip(lanes, ways)]
            came = [swap(goes, way[number]) for (goes, _), (way, _, _) in zip(parts, ways)]
            yield [goes for goes, _ in parts]
            came = self.take(came)
            lanes = [[stays, block] for (_, stays), block in zip(parts, came)]
        parts = [halves(terms, along[0]) for terms in lanes]
        cut = parts[0][0].shape[0]
        goes = jnp.concatenate([p[0] for p in parts], axis=0)
        stays = jnp.concatenate([p[1] for p in parts], axis=0)
        came = swap(goes, along[0])
        yield [goes]
        (came,) = self.take([came])
        mine = bfloat(widen(stays) + widen(came))
        for step in along[1:]:
            came = swap(mine, step)
            yield [mine]
            (came,) = self.take([came])
            mine = bfloat(widen(mine) + widen(came))
        came = swap(mine, along[0])
        yield [mine]
        (came,) = self.take([came])
        low, high = ordered(mine, came, along[0])
        lanes = [
            jnp.concatenate([low[n * cut : n * cut + cut], high[n * cut : n * cut + cut]], axis=0)
            for n in range(len(ways))
        ]
        for number in range(len(up) - 1, -1, -1):
            came = [swap(block, way[number]) for block, (way, _, _) in zip(lanes, ways)]
            yield lanes
            came = self.take(came)
            lanes = [
                jnp.concatenate(ordered(block, other, way[number]), axis=0)
                for block, other, (way, _, _) in zip(lanes, came, ways)
            ]
        block = lanes[0] if len(lanes) == 1 else jnp.concatenate(lanes, axis=0)
        came = swap(block, first)
        yield [block]
        return block, came


def entry_halves(block, step, bit):
    count = block.shape[0]
    grouped = block.reshape(count // (2 * bit), 2, bit, *block.shape[1:])
    side = side_of(step)
    take = lambda which: lax.dynamic_index_in_dim(grouped, which, 1, False).reshape(
        count // 2, *block.shape[1:]
    )
    return take(1 - side), take(side)


def shards(
    canvas,
    memory,
    cotangent,
    canvas_lengths,
    canvas_segments,
    memory_segments,
    memory_lengths,
    self_query,
    self_key,
    self_value,
    self_output,
    self_query_bias,
    self_value_bias,
    self_output_bias,
    first_gain,
    first_bias,
    cross_query,
    cross_key,
    cross_value,
    cross_output,
    cross_query_bias,
    cross_value_bias,
    cross_output_bias,
    second_gain,
    second_bias,
    expand_weight,
    expand_bias,
    reduce_weight,
    reduce_bias,
    third_gain,
    third_bias,
    slot_weight,
    slot_bias,
):
    place = lax.axis_index("seq")
    tokens_here = canvas.shape[1]
    width = canvas.shape[2]
    wide = expand_weight.shape[1]
    row = canvas[0]
    numbers = [
        jnp.stack([place, side_of(routes()[0])]).astype(jnp.int32),
        canvas_lengths, memory_lengths, canvas_segments,
    ]
    vectors, payload = pack(
        numbers,
        (
            self_query_bias, self_value_bias, self_output_bias, first_gain, first_bias,
            cross_query_bias, cross_value_bias, cross_output_bias, second_gain, second_bias,
            reduce_bias, third_gain, third_bias, slot_bias,
        ),
        expand_bias, canvas_segments, memory_segments, memory[0], row, cotangent[0],
    )
    side, middle = lax.ppermute(payload, "seq", SIDE), lax.ppermute(payload, "seq", MIDDLE)
    opposite = lax.ppermute(payload[tokens_here : tokens_here + TAIL], "seq", [(0, 3), (3, 0)])
    blocks = (
        payload, side, middle, lax.ppermute(side, "seq", MIDDLE), lax.ppermute(middle, "seq", OUTWARD)
    )
    last_memory = lax.ppermute(blocks[3][tokens_here + TAIL :], "seq", OUTWARD)
    projections = (self_query, self_key, self_value)

    queries, total, reach = self_near(numbers, canvas_segments, blocks, projections, vectors)
    blended, masses = self_far(
        numbers, canvas_segments, blocks, projections, vectors, queries, total, reach, opposite
    )
    (
        slots, last_slot, first_state, normal, scaling, low, cross_rows, fetched, cross_masses,
        second_grad, early_sums, gathered, early_sent, early_kept,
    ) = middle_forward(
        numbers, canvas_segments, row, blended, cotangent[0], vectors, blocks, last_memory,
        (self_output, cross_key, cross_value, cross_query, cross_output, expand_weight, reduce_weight, slot_weight),
    )
    order = Order()
    early = Summing(order, early_sent, early_kept, 2)
    early.step()
    first_grad, blended_grad, memory_part, later_sent, later_kept, later_sums = middle_backward(
        numbers, canvas_segments, blended, gathered, vectors,
        (normal, scaling, low, cross_rows, fetched, cross_masses, second_grad, first_state, masses),
        (self_output, cross_query, cross_key, cross_value, cross_output, self_value), order.last,
    )
    order.made(later_sums)
    early.step()
    later = Summing(order, later_sent, later_kept, LATER_SPLIT)
    far_part, *far = back_far(
        numbers, canvas_segments, blocks, projections, vectors, queries, blended, blended_grad, masses,
        opposite, order.last,
    )
    order.made(far[2])
    from_side = lax.ppermute(far_part, "seq", INWARD)
    from_middle = lax.ppermute(far_part, "seq", MIDDLE)
    near_step, far_step = routes()[3]
    memory_goes, memory_stays = entry_halves(memory_part, near_step, 1)
    memory_came = swap(memory_goes, near_step)
    early.step()
    (memory_came,) = order.after(memory_came)
    half_sum = bfloat(widen(memory_stays) + widen(memory_came))
    memory_goes, memory_stays = entry_halves(half_sum, far_step, 1)
    memory_came = swap(memory_goes, far_step)
    order.made(*order.last, memory_goes)
    later.step()
    canvas_base, middle_part, side_part, last_sent, last_kept = back_near(
        numbers, canvas_segments, blocks, projections, vectors, queries, blended, blended_grad, masses,
        first_grad, (early_sums, later_sums), far, order.last,
    )
    order.made(last_sent)
    last = Summing(order, last_sent, last_kept, LAST_SPLIT)
    finals = {}
    turns = {"E": early, "M": later, "S": last}
    for turn in TURNS:
        if turn in turns:
            turns[turn].step()
        elif turn == "1":
            from_side, from_middle = order.after(from_side, from_middle)
            middle_part = bfloat(widen(middle_part) + widen(from_side))
            side_part = bfloat(widen(side_part) + widen(from_middle))
            onward = lax.ppermute(middle_part, "seq", MIDDLE)
            outward = lax.ppermute(side_part, "seq", SIDE)
            order.made(middle_part, side_part)
        elif turn == "s":
            *self_grads, sums = unpack(
                numbers, "last_out", *last.finish(),
                [(width, [c * width]) for c in range(3)] + [(32, [3 * width])], order.last,
            )
            order.made(sums)
        elif turn == "e":
            count = 2 * width
            grad_slot, grad_expand, grad_reduce = unpack(
                numbers, "early_out", *early.finish(),
                [
                    (count, [0]),
                    (width, list(range(count, count + wide, width))),
                    (wide, [count + wide]),
                ],
                order.last,
            )
            order.made(grad_slot)
        elif turn == "m":
            cross_grads = unpack(
                numbers, "later_out", *later.finish(),
                [(width, [c * width]) for c in range(5)], order.last,
            )
            order.made(cross_grads[0])
        elif turn == "c":
            memory_grad, slots, canvas_grad = finish(
                numbers, memory_stays[0], memory_came[0], last_slot, slots, slot_weight[width:],
                canvas_base, onward, outward, order.last,
            )
            order.made(memory_grad)
    return (
        slots[None],
        canvas_grad[None],
        memory_grad[None],
        self_grads[0],
        self_grads[1],
        self_grads[2],
        cross_grads[4],
        sums[24],
        sums[25],
        sums[21],
        sums[19],
        sums[20],
        cross_grads[0],
        cross_grads[1],
        cross_grads[2],
        cross_grads[3],
        sums[17],
        sums[18],
        sums[16],
        sums[8],
        sums[9],
        grad_expand,
        sums[4:8].reshape(-1),
        grad_reduce,
        sums[3],
        sums[1],
        sums[2],
        grad_slot,
        sums[0],
    )


def solution(mesh):
    placed = (
        P("rows", "seq", None),
        P("rows", "seq", None),
        P("rows", "seq", None),
        P("rows"),
        P("rows", "seq"),
        P("rows", "seq"),
        P("rows"),
        P(),
        P(),
        P(),
        P(),
        P(),
        P(),
        P(),
        P(),
        P(),
        P(),
        P(),
        P(),
        P(),
        P(),
        P(),
        P(),
        P(),
        P(),
        P(),
        P(),
        P(),
        P(),
        P(),
        P(),
        P(),
        P(),
    )
    return jax.shard_map(
        shards,
        mesh=mesh,
        in_specs=placed,
        out_specs=(
            P("rows", "seq", None),
            P("rows", "seq", None),
            P("rows", "seq", None),
            P(),
            P(),
            P(),
            P(),
            P(),
            P(),
            P(),
            P(),
            P(),
            P(),
            P(),
            P(),
            P(),
            P(),
            P(),
            P(),
            P(),
            P(),
            P(),
            P(),
            P(),
            P(),
            P(),
            P(),
            P(),
            P(),
        ),
        check_vma=False,
    )
```

profile of v0, /device:TPU:9, one launch (start us, length us, event | category | flops | bytes accessed | tf_op | source)
XLA Modules:
  0.0 311.3 jit_solution(12445954308750370143)
XLA Ops:
  2.6 3.6 %pack.1 = (f32[18,512]{1,0:T(8,128)}, bf16[672,512]{1,0:T(8,128)(2,1)}) custom-call(s32[2]{0:T(128)} %pad_add_fusion.refs_0_, s32[1]{0:T(128)S(6)} %copy.65.refs_1_, s32[1]{0:T(128)S(6)} %copy.66.refs_2_, s32[1,512]{1,0:T(1,128)} %refs_3_.21, bf16[512,512]{1,0:T(8,128)(2,1)} %bitcast.53, bf16[512,512]{1,0:T(8,128)(2,1)} %bitcast.55, bf16[512]{0:T(512)(128)(2,1)} %refs_6_.3, ...), custom_call_target="tpu_custom_call" | custom-call | flops 2200000000 | tf_op jit(solution)/shard_map/pack/pallas_call | solution.py:611
  6.3 4.5 %collective-permute-start.1 = (bf16[672,512]{1,0:T(8,128)(2,1)}, bf16[672,512]{1,0:T(8,128)(2,1)S(1)}, u32[]{:S(2)}, u32[]{:S(2)}) collective-permute-start(bf16[672,512]{1,0:T(8,128)(2,1)} %get-tuple-element.115.refs_4_), channel_id=1, source_target_pairs={{1,2},{2,1},{5,6},{6,5},{9,10},{10,9},{13,14},{14,13},{17,18},{18,... | collective-permute-start | bytes 2064392 | tf_op jit(solution)/shard_map/ppermute | solution.py:1468
  12.1 10.6 %collective-permute-done.refs_5_ = bf16[672,512]{1,0:T(8,128)(2,1)S(1)} collective-permute-done((bf16[672,512]{1,0:T(8,128)(2,1)}, bf16[672,512]{1,0:T(8,128)(2,1)S(1)}, u32[]{:S(2)}, u32[]{:S(2)}) %collective-permute-start) | collective-permute-done | bytes 688160 | tf_op jit(solution)/shard_map/ppermute | solution.py:1468
  22.8 3.2 %collective-permute-start.2 = (bf16[672,512]{1,0:T(8,128)(2,1)S(1)}, bf16[672,512]{1,0:T(8,128)(2,1)S(1)}, u32[]{:S(2)}, u32[]{:S(2)}) collective-permute-start(bf16[672,512]{1,0:T(8,128)(2,1)S(1)} %collective-permute-done.refs_5_), channel_id=1, source_target_pairs={{1,2},{2,1},{5,6},{6,5},{9,10},{10,9},{13,14},{14,13},{17,18},{18,... | collective-permute-start | bytes 2064392 | tf_op jit(solution)/shard_map/ppermute | solution.py:1471
  27.5 15.9 %self_near.1 = (bf16[512,512]{1,0:T(8,128)(2,1)}, f32[8,80,512]{2,1,0:T(8,128)}, f32[16,128]{1,0:T(8,128)}) custom-call(s32[2]{0:T(128)} %pad_add_fusion.refs_0_, s32[1]{0:T(128)S(6)} %copy.65.refs_1_, s32[1]{0:T(128)S(6)} %copy.66.refs_2_, s32[1,512]{1,0:T(1,128)} %refs_3_.21, bf16[672,512]{1,0:T(8,128)(2,1)} %get-tuple-element.115.refs_4_, ...), custom_call_target="tpu_custom_call" | custom-call | flops 14300000256 | tf_op jit(solution)/shard_map/self_near/pallas_call | solution.py:611
  45.6 4.7 %self_far.1 = (bf16[512,512]{1,0:T(8,128)(2,1)}, f32[8,512]{1,0:T(8,128)}) custom-call(s32[2]{0:T(128)} %pad_add_fusion.refs_0_, s32[1]{0:T(128)S(6)} %copy.65.refs_1_, s32[1]{0:T(128)S(6)} %copy.66.refs_2_, s32[1,512]{1,0:T(1,128)} %refs_3_.21, bf16[672,512]{1,0:T(8,128)(2,1)} %get-tuple-element.115.refs_4_, bf16[672,512]{1,0:T(8,128)(2,1)} %copy-done.18, ...), custom_call_target="tpu_custom_call" | custom-call | flops 7699999744 | tf_op jit(solution)/shard_map/self_far/pallas_call | solution.py:611
  51.0 25.8 %middle_forward.1 = (bf16[512,512]{1,0:T(8,128)(2,1)}, f32[8,512]{1,0:T(8,128)}, bf16[16,512]{1,0:T(8,128)(2,1)}, f32[512,512]{1,0:T(8,128)}, f32[512,128]{1,0:T...) custom-call(s32[2]{0:T(128)} %pad_add_fusion.refs_0_, ...), custom_call_target="tpu_custom_call" | custom-call | flops 26400000000 | tf_op jit(solution)/shard_map/middle_forward/pallas_call | solution.py:611
  76.7 7.5 %collective-permute-start.6 = (bf16[2560,512]{1,0:T(8,128)(2,1)}, bf16[2560,512]{1,0:T(8,128)(2,1)S(1)}, u32[]{:S(2)}, u32[]{:S(2)}) collective-permute-start(bf16[2560,512]{1,0:T(8,128)(2,1)} %get-tuple-element.132), channel_id=1, source_target_pairs={{0,4},{4,0},{8,12},{12,8},{16,20},{20,16},{24,28},{28,24},{1,5},{5... | collective-permute-start | bytes 7864328 | tf_op jit(solution)/shard_map/ppermute | solution.py:1291
  86.1 2.9 collective-permute-done.6
  89.6 23.8 %collective-permute-start.8 = (bf16[640,512]{1,0:T(8,128)(2,1)S(1)}, bf16[640,512]{1,0:T(8,128)(2,1)S(1)}, u32[]{:S(2)}, u32[]{:S(2)}) collective-permute-start(bf16[640,512]{1,0:T(8,128)(2,1)S(1)} %get-tuple-element.206.refs_23_), channel_id=1, source_target_pairs={{0,8},{4,12},{8,0},{12,4},{16,24},{20,28},{24,16},{28,20},{1,9},{5... | collective-permute-start | bytes 1966088 | tf_op jit(solution)/shard_map/ppermute | solution.py:1291
  113.8 6.1 %collective-permute-start.9 = (bf16[640,512]{1,0:T(8,128)(2,1)S(1)}, bf16[640,512]{1,0:T(8,128)(2,1)S(1)}, u32[]{:S(2)}, u32[]{:S(2)}) collective-permute-start(bf16[640,512]{1,0:T(8,128)(2,1)S(1)} %get-tuple-element.204.refs_24_), channel_id=1, source_target_pairs={{0,16},{4,20},{8,24},{12,28},{16,0},{20,4},{24,8},{28,12},{1,17},{... | collective-permute-start | bytes 1966088 | tf_op jit(solution)/shard_map/ppermute | solution.py:1291
  119.9 17.2 %middle_backward.1 = (f32[512,512]{1,0:T(8,128)}, bf16[512,512]{1,0:T(8,128)(2,1)}, bf16[4,144,512]{2,1,0:T(8,128)(2,1)}, bf16[1280,512]{1,0:T(8,128)(2,1)}, bf1...) custom-call(s32[2]{0:T(128)} %pad_add_fusion.refs_0_, s32[1]{0:T(128)S(6)} %copy.65.refs_1_, s32[1]{0:T(128)S(6)} %copy.66.refs_2_, ...), custom_call_target="tpu_custom_call" | custom-call | flops 17600000000 | tf_op jit(solution)/shard_map/middle_backward/pallas_call | solution.py:611
  141.4 4.9 %back_far.1 = (bf16[512,512]{1,0:T(8,128)(2,1)}, f32[512,512]{1,0:T(8,128)}, f32[512,512]{1,0:T(8,128)}, f32[8,512]{1,0:T(8,128)}, f32[512,512]{1,0:T(8,128)}) custom-call(s32[2]{0:T(128)} %pad_add_fusion.refs_0_, s32[1]{0:T(128)S(6)} %copy.65.refs_1_, s32[1]{0:T(128)S(6)} %copy.66.refs_2_, s32[1,512]{1,0:T(1,128)} %refs_3_.21, bf16[672,512]{1,0:T(8,128)(2,1)} %copy-done.15, ...), custom_call_target="tpu_custom_call" | custom-call | flops 8800000000 | tf_op jit(solution)/shard_map/back_far/pallas_call | solution.py:611
  149.3 2.6 collective-permute-start.15
  156.0 25.9 %back_near.1 = (f32[512,512]{1,0:T(8,128)}, bf16[512,512]{1,0:T(8,128)(2,1)}, bf16[512,512]{1,0:T(8,128)(2,1)}, bf16[896,512]{1,0:T(8,128)(2,1)}, bf16[896,512]{1,0:T(8,128)(2,1)}) custom-call(s32[2]{0:T(128)} %pad_add_fusion.refs_0_, s32[1]{0:T(128)S(6)} %copy.65.refs_1_, s32[1]{0:T(128)S(6)} %copy.66.refs_2_, s32[1,512]{1,0:T(1,128)} %refs_3_.21, ...), custom_call_target="tpu_custom_call" | custom-call | flops 24199999488 | tf_op jit(solution)/shard_map/back_near/pallas_call | solution.py:611
  181.9 12.8 %collective-permute-start.21 = (bf16[896,512]{1,0:T(8,128)(2,1)}, bf16[896,512]{1,0:T(8,128)(2,1)S(1)}, u32[]{:S(2)}, u32[]{:S(2)}) collective-permute-start(bf16[896,512]{1,0:T(8,128)(2,1)} %get-tuple-element.155), channel_id=1, source_target_pairs={{0,4},{4,0},{8,12},{12,8},{16,20},{20,16},{24,28},{28,24},{1,5},{5... | collective-permute-start | bytes 2752520 | tf_op jit(solution)/shard_map/ppermute | solution.py:1291
  199.0 6.7 %collective-permute-done.20 = bf16[320,512]{1,0:T(8,128)(2,1)} collective-permute-done((bf16[320,512]{1,0:T(8,128)(2,1)S(1)}, bf16[320,512]{1,0:T(8,128)(2,1)}, u32[]{:S(2)}, u32[]{:S(2)}) %collective-permute-start.20) | collective-permute-done | bytes 327712 | tf_op jit(solution)/shard_map/ppermute | solution.py:1291
  206.8 3.9 %collective-permute-done.25 = bf16[224,512]{1,0:T(8,128)(2,1)} collective-permute-done((bf16[224,512]{1,0:T(8,128)(2,1)S(1)}, bf16[224,512]{1,0:T(8,128)(2,1)}, u32[]{:S(2)}, u32[]{:S(2)}) %collective-permute-start.25) | collective-permute-done | bytes 229408 | tf_op jit(solution)/shard_map/ppermute | solution.py:1291
  213.6 2.2 collective-permute-start.30
  218.5 5.8 %collective-permute-done.30 = bf16[320,512]{1,0:T(8,128)(2,1)S(1)} collective-permute-done((bf16[320,512]{1,0:T(8,128)(2,1)S(1)}, bf16[320,512]{1,0:T(8,128)(2,1)S(1)}, u32[]{:S(2)}, u32[]{:S(2)}) %collective-permute-start.30) | collective-permute-done | bytes 327712 | tf_op jit(solution)/shard_map/ppermute | solution.py:1291
  226.2 2.3 collective-permute-done.29
  231.4 3.5 %collective-permute-done.31 = bf16[160,512]{1,0:T(8,128)(2,1)S(1)} collective-permute-done((bf16[160,512]{1,0:T(8,128)(2,1)S(1)}, bf16[160,512]{1,0:T(8,128)(2,1)S(1)}, u32[]{:S(2)}, u32[]{:S(2)}) %collective-permute-start.31) | collective-permute-done | bytes 163872 | tf_op jit(solution)/shard_map/ppermute | solution.py:1291
  238.2 2.0 collective-permute-done.36
  240.3 6.7 %collective-permute-done.39 = bf16[640,512]{1,0:T(8,128)(2,1)S(1)} collective-permute-done((bf16[640,512]{1,0:T(8,128)(2,1)S(1)}, bf16[640,512]{1,0:T(8,128)(2,1)S(1)}, u32[]{:S(2)}, u32[]{:S(2)}) %collective-permute-start.39) | collective-permute-done | bytes 655392 | tf_op jit(solution)/shard_map/ppermute | solution.py:1291
  249.0 5.8 %collective-permute-start.43 = (bf16[2560,512]{1,0:T(8,128)(2,1)S(1)}, bf16[2560,512]{1,0:T(8,128)(2,1)}, u32[]{:S(2)}, u32[]{:S(2)}) collective-permute-start(bf16[2560,512]{1,0:T(8,128)(2,1)S(1)} %pad_maximum_fusion.refs_4_), channel_id=1, source_target_pairs={{0,4},{4,0},{8,12},{12,8},{16,20},{20,16},{24,28},{28,24},{1,5},{5... | collective-permute-start | bytes 7864328 | tf_op jit(solution)/shard_map/ppermute | solution.py:1291
  257.6 4.0 %collective-permute-start.18 = (bf16[512,512]{1,0:T(8,128)(2,1)S(1)}, bf16[512,512]{1,0:T(8,128)(2,1)S(1)}, u32[]{:S(2)}, u32[]{:S(2)}) collective-permute-start(bf16[512,512]{1,0:T(8,128)(2,1)S(1)} %add_convert_fusion.7), channel_id=1, source_target_pairs={{1,2},{2,1},{5,6},{6,5},{9,10},{10,9},{13,14},{14,13},{17,18},{18,... | collective-permute-start | bytes 1572872 | tf_op jit(solution)/shard_map/ppermute | solution.py:1530
  262.5 7.2 %collective-permute-done.34 = bf16[320,512]{1,0:T(8,128)(2,1)S(1)} collective-permute-done((bf16[320,512]{1,0:T(8,128)(2,1)S(1)}, bf16[320,512]{1,0:T(8,128)(2,1)S(1)}, u32[]{:S(2)}, u32[]{:S(2)}) %collective-permute-start.34) | collective-permute-done | bytes 327712 | tf_op jit(solution)/shard_map/ppermute | solution.py:1291
  271.5 6.9 %collective-permute-done.18.refs_10_ = bf16[512,512]{1,0:T(8,128)(2,1)S(1)} collective-permute-done((bf16[512,512]{1,0:T(8,128)(2,1)S(1)}, bf16[512,512]{1,0:T(8,128)(2,1)S(1)}, u32[]{:S(2)}, u32[]{:S(2)}) %collective-permute-start.18) | collective-permute-done | bytes 524320 | tf_op jit(solution)/shard_map/ppermute | solution.py:1530
  280.5 3.9 %finish.1 = (f32[128,512]{1,0:T(8,128)}, bf16[512,512]{1,0:T(8,128)(2,1)}, f32[512,512]{1,0:T(8,128)}) custom-call(s32[2]{0:T(128)} %pad_add_fusion.refs_0_, s32[1]{0:T(128)S(6)} %copy.65.refs_1_, s32[1]{0:T(128)S(6)} %copy.66.refs_2_, s32[1,512]{1,0:T(1,128)} %refs_3_.21, bf16[144,512]{1,0:T(8,128)(2,1)} %get-tuple-element.258.refs_4_, ...), custom_call_target="tpu_custom_call" | custom-call | flops 3300000000 | tf_op jit(solution)/shard_map/finish/pallas_call | solution.py:611
  284.4 7.5 %early_out.1 = (f32[1024,512]{1,0:T(8,128)}, f32[512,2048]{1,0:T(8,128)}, f32[2048,512]{1,0:T(8,128)}) custom-call(s32[2]{0:T(128)} %pad_add_fusion.refs_0_, s32[1]{0:T(128)S(6)} %copy.65.refs_1_, s32[1]{0:T(128)S(6)} %copy.66.refs_2_, s32[1,512]{1,0:T(1,128)} %refs_3_.21, bf16[2560,512]{1,0:T(8,128)(2,1)} %copy-done, ...), custom_call_target="tpu_custom_call" | custom-call | flops 4400000000 | tf_op jit(solution)/shard_map/early_out/pallas_call | solution.py:611
  298.0 3.9 %last_out.1 = (f32[512,512]{1,0:T(8,128)}, f32[512,512]{1,0:T(8,128)}, f32[512,512]{1,0:T(8,128)}, f32[32,512]{1,0:T(8,128)}) custom-call(s32[2]{0:T(128)} %pad_add_fusion.refs_0_, s32[1]{0:T(128)S(6)} %copy.65.refs_1_, s32[1]{0:T(128)S(6)} %copy.66.refs_2_, s32[1,512]{1,0:T(1,128)} %refs_3_.21, bf16[896,512]{1,0:T(8,128)(2,1)} %copy-done.3, ...), custom_call_target="tpu_custom_call" | custom-call | flops 4400000000 | tf_op jit(solution)/shard_map/last_out/pallas_call | solution.py:611
  305.9 4.9 %later_out.1 = (f32[512,512]{1,0:T(8,128)}, f32[512,512]{1,0:T(8,128)}, f32[512,512]{1,0:T(8,128)}, f32[512,512]{1,0:T(8,128)}, f32[512,512]{1,0:T(8,128)}) custom-call(s32[2]{0:T(128)} %pad_add_fusion.refs_0_, s32[1]{0:T(128)S(6)} %copy.65.refs_1_, s32[1]{0:T(128)S(6)} %copy.66.refs_2_, s32[1,512]{1,0:T(1,128)} %refs_3_.21, bf16[1280,512]{1,0:T(8,128)(2,1)} %copy-done.2, ...), custom_call_target="tpu_custom_call" | custom-call | flops 4400000000 | tf_op jit(solution)/shard_map/later_out/pallas_call | solution.py:611
  (193 shorter events, 58.9 us)
Async XLA Ops:
  6.2 16.6 %collective-permute-start = (bf16[672,512]{1,0:T(8,128)(2,1)}, bf16[672,512]{1,0:T(8,128)(2,1)S(1)}, u32[]{:S(2)}, u32[]{:S(2)}) collective-permute-start(bf16[672,512]{1,0:T(8,128)(2,1)} %get-tuple-element.115.refs_4_), channel_id=1, source_target_pairs={{0,1},{1,0},{2,3},{3,2},{4,5},{5,4},{6,7},{7,6},{8,9},{9,8},{10,11... | collective-permute-start | bytes 2064392 | tf_op jit(solution)/shard_map/ppermute | solution.py:1468
  6.3 19.9 %collective-permute-start.1 = (bf16[672,512]{1,0:T(8,128)(2,1)}, bf16[672,512]{1,0:T(8,128)(2,1)S(1)}, u32[]{:S(2)}, u32[]{:S(2)}) collective-permute-start(bf16[672,512]{1,0:T(8,128)(2,1)} %get-tuple-element.115.refs_4_), channel_id=1, source_target_pairs={{1,2},{2,1},{5,6},{6,5},{9,10},{10,9},{13,14},{14,13},{17,18},{18,... | collective-permute-start | bytes 2064392 | tf_op jit(solution)/shard_map/ppermute | solution.py:1468
  11.5 33.2 %collective-permute-start.5 = (bf16[16,512]{1,0:T(8,128)(2,1)S(1)}, bf16[16,512]{1,0:T(8,128)(2,1)S(1)}, u32[]{:S(2)}, u32[]{:S(2)}) collective-permute-start(bf16[16,512]{1,0:T(8,128)(2,1)S(1)} %slice.103), channel_id=1, source_target_pairs={{0,3},{3,0},{4,7},{7,4},{8,11},{11,8},{12,15},{15,12},{16,19},{19,... | collective-permute-start | bytes 49160 | tf_op jit(solution)/shard_map/ppermute | solution.py:1469
  22.8 20.6 %collective-permute-start.2 = (bf16[672,512]{1,0:T(8,128)(2,1)S(1)}, bf16[672,512]{1,0:T(8,128)(2,1)S(1)}, u32[]{:S(2)}, u32[]{:S(2)}) collective-permute-start(bf16[672,512]{1,0:T(8,128)(2,1)S(1)} %collective-permute-done.refs_5_), channel_id=1, source_target_pairs={{1,2},{2,1},{5,6},{6,5},{9,10},{10,9},{13,14},{14,13},{17,18},{18,... | collective-permute-start | bytes 2064392 | tf_op jit(solution)/shard_map/ppermute | solution.py:1471
  26.1 18.6 %collective-permute-start.3 = (bf16[672,512]{1,0:T(8,128)(2,1)S(1)}, bf16[672,512]{1,0:T(8,128)(2,1)S(1)}, u32[]{:S(2)}, u32[]{:S(2)}) collective-permute-start(bf16[672,512]{1,0:T(8,128)(2,1)S(1)} %collective-permute-done.1.refs_6_), channel_id=1, source_target_pairs={{1,0},{2,3},{5,4},{6,7},{9,8},{10,11},{13,12},{14,15},{17,16},{18,... | collective-permute-start | bytes 2064392 | tf_op jit(solution)/shard_map/ppermute | solution.py:1471
  76.7 12.3 %collective-permute-start.6 = (bf16[2560,512]{1,0:T(8,128)(2,1)}, bf16[2560,512]{1,0:T(8,128)(2,1)S(1)}, u32[]{:S(2)}, u32[]{:S(2)}) collective-permute-start(bf16[2560,512]{1,0:T(8,128)(2,1)} %get-tuple-element.132), channel_id=1, source_target_pairs={{0,4},{4,0},{8,12},{12,8},{16,20},{20,16},{24,28},{28,24},{1,5},{5... | collective-permute-start | bytes 7864328 | tf_op jit(solution)/shard_map/ppermute | solution.py:1291
  89.6 50.2 %collective-permute-start.8 = (bf16[640,512]{1,0:T(8,128)(2,1)S(1)}, bf16[640,512]{1,0:T(8,128)(2,1)S(1)}, u32[]{:S(2)}, u32[]{:S(2)}) collective-permute-start(bf16[640,512]{1,0:T(8,128)(2,1)S(1)} %get-tuple-element.206.refs_23_), channel_id=1, source_target_pairs={{0,8},{4,12},{8,0},{12,4},{16,24},{20,28},{24,16},{28,20},{1,9},{5... | collective-permute-start | bytes 1966088 | tf_op jit(solution)/shard_map/ppermute | solution.py:1291
  113.8 25.9 %collective-permute-start.9 = (bf16[640,512]{1,0:T(8,128)(2,1)S(1)}, bf16[640,512]{1,0:T(8,128)(2,1)S(1)}, u32[]{:S(2)}, u32[]{:S(2)}) collective-permute-start(bf16[640,512]{1,0:T(8,128)(2,1)S(1)} %get-tuple-element.204.refs_24_), channel_id=1, source_target_pairs={{0,16},{4,20},{8,24},{12,28},{16,0},{20,4},{24,8},{28,12},{1,17},{... | collective-permute-start | bytes 1966088 | tf_op jit(solution)/shard_map/ppermute | solution.py:1291
  138.8 13.4 %collective-permute-start.7 = (bf16[2,144,512]{2,1,0:T(8,128)(2,1)}, bf16[2,144,512]{2,1,0:T(8,128)(2,1)}, u32[]{:S(2)}, u32[]{:S(2)}) collective-permute-start(bf16[2,144,512]{2,1,0:T(8,128)(2,1)} %dynamic-slice_bitcast_fusion), channel_id=1, source_target_pairs={{0,1},{1,0},{2,3},{3,2},{4,5},{5,4},{6,7},{7,6},{8,9},{9,8},{10,11... | collective-permute-start | bytes 884744 | tf_op jit(solution)/shard_map/ppermute | solution.py:1291
  138.8 15.9 %collective-permute-start.13 = (bf16[1280,512]{1,0:T(8,128)(2,1)}, bf16[1280,512]{1,0:T(8,128)(2,1)S(1)}, u32[]{:S(2)}, u32[]{:S(2)}) collective-permute-start(bf16[1280,512]{1,0:T(8,128)(2,1)} %get-tuple-element.150), channel_id=1, source_target_pairs={{0,4},{4,0},{8,12},{12,8},{16,20},{20,16},{24,28},{28,24},{1,5},{5... | collective-permute-start | bytes 3932168 | tf_op jit(solution)/shard_map/ppermute | solution.py:1291
  140.7 11.2 %collective-permute-start.11 = (bf16[320,512]{1,0:T(8,128)(2,1)S(1)}, bf16[320,512]{1,0:T(8,128)(2,1)S(1)}, u32[]{:S(2)}, u32[]{:S(2)}) collective-permute-start(bf16[320,512]{1,0:T(8,128)(2,1)S(1)} %get-tuple-element.222.refs_16_), channel_id=1, source_target_pairs={{0,8},{4,12},{8,0},{12,4},{16,24},{20,28},{24,16},{28,20},{1,9},{5... | collective-permute-start | bytes 983048 | tf_op jit(solution)/shard_map/ppermute | solution.py:1291
  146.2 50.1 %collective-permute-start.14 = (bf16[512,512]{1,0:T(8,128)(2,1)}, bf16[512,512]{1,0:T(8,128)(2,1)S(1)}, u32[]{:S(2)}, u32[]{:S(2)}) collective-permute-start(bf16[512,512]{1,0:T(8,128)(2,1)} %get-tuple-element.154), channel_id=1, source_target_pairs={{0,1},{3,2},{4,5},{7,6},{8,9},{11,10},{12,13},{15,14},{16,17},{19,... | collective-permute-start | bytes 1572872 | tf_op jit(solution)/shard_map/ppermute | solution.py:1503
  149.3 47.0 %collective-permute-start.15 = (bf16[512,512]{1,0:T(8,128)(2,1)}, bf16[512,512]{1,0:T(8,128)(2,1)S(1)}, u32[]{:S(2)}, u32[]{:S(2)}) collective-permute-start(bf16[512,512]{1,0:T(8,128)(2,1)} %get-tuple-element.154), channel_id=1, source_target_pairs={{1,2},{2,1},{5,6},{6,5},{9,10},{10,9},{13,14},{14,13},{17,18},{18,... | collective-permute-start | bytes 1572872 | tf_op jit(solution)/shard_map/ppermute | solution.py:1504
  152.2 43.7 %collective-permute-start.17 = (bf16[320,512]{1,0:T(8,128)(2,1)S(1)}, bf16[320,512]{1,0:T(8,128)(2,1)S(1)}, u32[]{:S(2)}, u32[]{:S(2)}) collective-permute-start(bf16[320,512]{1,0:T(8,128)(2,1)S(1)} %pad_maximum_fusion.6), channel_id=1, source_target_pairs={{0,1},{1,0},{2,3},{3,2},{4,5},{5,4},{6,7},{7,6},{8,9},{9,8},{10,11... | collective-permute-start | bytes 983048 | tf_op jit(solution)/shard_map/ppermute | solution.py:1291
  155.2 40.8 %collective-permute-start.16 = (bf16[640,512]{1,0:T(8,128)(2,1)S(1)}, bf16[640,512]{1,0:T(8,128)(2,1)S(1)}, u32[]{:S(2)}, u32[]{:S(2)}) collective-permute-start(bf16[640,512]{1,0:T(8,128)(2,1)S(1)} %get-tuple-element.202.refs_23_), channel_id=1, source_target_pairs={{0,8},{4,12},{8,0},{12,4},{16,24},{20,28},{24,16},{28,20},{1,9},{5... | collective-permute-start | bytes 1966088 | tf_op jit(solution)/shard_map/ppermute | solution.py:1291
  181.9 15.4 %collective-permute-start.21 = (bf16[896,512]{1,0:T(8,128)(2,1)}, bf16[896,512]{1,0:T(8,128)(2,1)S(1)}, u32[]{:S(2)}, u32[]{:S(2)}) collective-permute-start(bf16[896,512]{1,0:T(8,128)(2,1)} %get-tuple-element.155), channel_id=1, source_target_pairs={{0,4},{4,0},{8,12},{12,8},{16,20},{20,16},{24,28},{28,24},{1,5},{5... | collective-permute-start | bytes 2752520 | tf_op jit(solution)/shard_map/ppermute | solution.py:1291
  196.2 9.5 %collective-permute-start.20 = (bf16[320,512]{1,0:T(8,128)(2,1)S(1)}, bf16[320,512]{1,0:T(8,128)(2,1)}, u32[]{:S(2)}, u32[]{:S(2)}) collective-permute-start(bf16[320,512]{1,0:T(8,128)(2,1)S(1)} %get-tuple-element.218), channel_id=1, source_target_pairs={{0,16},{4,20},{8,24},{12,28},{16,0},{20,4},{24,8},{28,12},{1,17},{... | collective-permute-start | bytes 983048 | tf_op jit(solution)/shard_map/ppermute | solution.py:1291
  198.2 12.5 %collective-permute-start.25 = (bf16[224,512]{1,0:T(8,128)(2,1)S(1)}, bf16[224,512]{1,0:T(8,128)(2,1)}, u32[]{:S(2)}, u32[]{:S(2)}) collective-permute-start(bf16[224,512]{1,0:T(8,128)(2,1)S(1)} %get-tuple-element.224), channel_id=1, source_target_pairs={{0,16},{4,20},{8,24},{12,28},{16,0},{20,4},{24,8},{28,12},{1,17},{... | collective-permute-start | bytes 688136 | tf_op jit(solution)/shard_map/ppermute | solution.py:1291
  199.0 14.5 %collective-permute-start.23 = (bf16[320,512]{1,0:T(8,128)(2,1)S(1)}, bf16[320,512]{1,0:T(8,128)(2,1)S(1)}, u32[]{:S(2)}, u32[]{:S(2)}) collective-permute-start(bf16[320,512]{1,0:T(8,128)(2,1)S(1)} %add_convert_fusion.11), channel_id=1, source_target_pairs={{0,2},{1,3},{2,0},{3,1},{4,6},{5,7},{6,4},{7,5},{8,10},{9,11},{10,... | collective-permute-start | bytes 983048 | tf_op jit(solution)/shard_map/ppermute | solution.py:1291
  213.6 10.8 %collective-permute-start.30 = (bf16[320,512]{1,0:T(8,128)(2,1)S(1)}, bf16[320,512]{1,0:T(8,128)(2,1)S(1)}, u32[]{:S(2)}, u32[]{:S(2)}) collective-permute-start(bf16[320,512]{1,0:T(8,128)(2,1)S(1)} %add_convert_fusion.8), channel_id=1, source_target_pairs={{0,1},{1,0},{2,3},{3,2},{4,5},{5,4},{6,7},{7,6},{8,9},{9,8},{10,11... | collective-permute-start | bytes 983048 | tf_op jit(solution)/shard_map/ppermute | solution.py:1291
  216.7 13.6 %collective-permute-start.26 = (bf16[160,512]{1,0:T(8,128)(2,1)S(1)}, bf16[160,512]{1,0:T(8,128)(2,1)S(1)}, u32[]{:S(2)}, u32[]{:S(2)}) collective-permute-start(bf16[160,512]{1,0:T(8,128)(2,1)S(1)} %add_convert_fusion.21), channel_id=1, source_target_pairs={{0,2},{1,3},{2,0},{3,1},{4,6},{5,7},{6,4},{7,5},{8,10},{9,11},{10,... | collective-permute-start | bytes 491528 | tf_op jit(solution)/shard_map/ppermute | solution.py:1291
  217.4 11.1 %collective-permute-start.29 = (bf16[112,512]{1,0:T(8,128)(2,1)S(1)}, bf16[112,512]{1,0:T(8,128)(2,1)S(1)}, u32[]{:S(2)}, u32[]{:S(2)}) collective-permute-start(bf16[112,512]{1,0:T(8,128)(2,1)S(1)} %pad_maximum_fusion.12), channel_id=1, source_target_pairs={{0,1},{1,0},{2,3},{3,2},{4,5},{5,4},{6,7},{7,6},{8,9},{9,8},{10,11... | collective-permute-start | bytes 344072 | tf_op jit(solution)/shard_map/ppermute | solution.py:1291
  236.3 10.7 %collective-permute-start.39 = (bf16[640,512]{1,0:T(8,128)(2,1)S(1)}, bf16[640,512]{1,0:T(8,128)(2,1)S(1)}, u32[]{:S(2)}, u32[]{:S(2)}) collective-permute-start(bf16[640,512]{1,0:T(8,128)(2,1)S(1)} %pad_maximum_fusion.3), channel_id=1, source_target_pairs={{0,8},{4,12},{8,0},{12,4},{16,24},{20,28},{24,16},{28,20},{1,9},{5... | collective-permute-start | bytes 1966088 | tf_op jit(solution)/shard_map/ppermute | solution.py:1291
  236.3 11.9 %collective-permute-start.40 = (bf16[640,512]{1,0:T(8,128)(2,1)S(1)}, bf16[640,512]{1,0:T(8,128)(2,1)S(1)}, u32[]{:S(2)}, u32[]{:S(2)}) collective-permute-start(bf16[640,512]{1,0:T(8,128)(2,1)S(1)} %pad_maximum_fusion.4), channel_id=1, source_target_pairs={{0,16},{4,20},{8,24},{12,28},{16,0},{20,4},{24,8},{28,12},{1,17},{... | collective-permute-start | bytes 1966088 | tf_op jit(solution)/shard_map/ppermute | solution.py:1291
  249.0 35.4 %collective-permute-start.43 = (bf16[2560,512]{1,0:T(8,128)(2,1)S(1)}, bf16[2560,512]{1,0:T(8,128)(2,1)}, u32[]{:S(2)}, u32[]{:S(2)}) collective-permute-start(bf16[2560,512]{1,0:T(8,128)(2,1)S(1)} %pad_maximum_fusion.refs_4_), channel_id=1, source_target_pairs={{0,4},{4,0},{8,12},{12,8},{16,20},{20,16},{24,28},{28,24},{1,5},{5... | collective-permute-start | bytes 7864328 | tf_op jit(solution)/shard_map/ppermute | solution.py:1291
  257.2 14.2 %collective-permute-start.12 = (bf16[1,144,512]{2,1,0:T(8,128)(2,1)S(1)}, bf16[1,144,512]{2,1,0:T(8,128)(2,1)S(1)}, u32[]{:S(2)}, u32[]{:S(2)}) collective-permute-start(bf16[1,144,512]{2,1,0:T(8,128)(2,1)S(1)} %copy-done.14), channel_id=1, source_target_pairs={{0,2},{1,3},{2,0},{3,1},{4,6},{5,7},{6,4},{7,5},{8,10},{9,11},{10,... | collective-permute-start | bytes 442376 | tf_op jit(solution)/shard_map/ppermute | solution.py:1291
  257.6 20.8 %collective-permute-start.18 = (bf16[512,512]{1,0:T(8,128)(2,1)S(1)}, bf16[512,512]{1,0:T(8,128)(2,1)S(1)}, u32[]{:S(2)}, u32[]{:S(2)}) collective-permute-start(bf16[512,512]{1,0:T(8,128)(2,1)S(1)} %add_convert_fusion.7), channel_id=1, source_target_pairs={{1,2},{2,1},{5,6},{6,5},{9,10},{10,9},{13,14},{14,13},{17,18},{18,... | collective-permute-start | bytes 1572872 | tf_op jit(solution)/shard_map/ppermute | solution.py:1530
  261.6 18.1 %collective-permute-start.19 = (bf16[512,512]{1,0:T(8,128)(2,1)S(1)}, bf16[512,512]{1,0:T(8,128)(2,1)S(1)}, u32[]{:S(2)}, u32[]{:S(2)}) collective-permute-start(bf16[512,512]{1,0:T(8,128)(2,1)S(1)} %add_convert_fusion.6), channel_id=1, source_target_pairs={{0,1},{1,0},{2,3},{3,2},{4,5},{5,4},{6,7},{7,6},{8,9},{9,8},{10,11... | collective-permute-start | bytes 1572872 | tf_op jit(solution)/shard_map/ppermute | solution.py:1531
  269.8 22.2 %collective-permute-start.41 = (bf16[224,512]{1,0:T(8,128)(2,1)S(1)}, bf16[224,512]{1,0:T(8,128)(2,1)}, u32[]{:S(2)}, u32[]{:S(2)}) collective-permute-start(bf16[224,512]{1,0:T(8,128)(2,1)S(1)} %pad_maximum_fusion.10), channel_id=1, source_target_pairs={{0,8},{4,12},{8,0},{12,4},{16,24},{20,28},{24,16},{28,20},{1,9},{5... | collective-permute-start | bytes 688136 | tf_op jit(solution)/shard_map/ppermute | solution.py:1291
  271.4 20.5 %collective-permute-start.42 = (bf16[224,512]{1,0:T(8,128)(2,1)S(1)}, bf16[224,512]{1,0:T(8,128)(2,1)}, u32[]{:S(2)}, u32[]{:S(2)}) collective-permute-start(bf16[224,512]{1,0:T(8,128)(2,1)S(1)} %pad_maximum_fusion.11), channel_id=1, source_target_pairs={{0,16},{4,20},{8,24},{12,28},{16,0},{20,4},{24,8},{28,12},{1,17},{... | collective-permute-start | bytes 688136 | tf_op jit(solution)/shard_map/ppermute | solution.py:1291
  278.4 16.5 %collective-permute-start.45 = (bf16[640,512]{1,0:T(8,128)(2,1)S(1)}, bf16[640,512]{1,0:T(8,128)(2,1)S(1)}, u32[]{:S(2)}, u32[]{:S(2)}) collective-permute-start(bf16[640,512]{1,0:T(8,128)(2,1)S(1)} %pad_maximum_fusion.5.refs_12_), channel_id=1, source_target_pairs={{0,8},{4,12},{8,0},{12,4},{16,24},{20,28},{24,16},{28,20},{1,9},{5... | collective-permute-start | bytes 1966088 | tf_op jit(solution)/shard_map/ppermute | solution.py:1291
  295.3 9.5 %collective-permute-start.46 = (bf16[1280,512]{1,0:T(8,128)(2,1)S(1)}, bf16[1280,512]{1,0:T(8,128)(2,1)S(1)}, u32[]{:S(2)}, u32[]{:S(2)}) collective-permute-start(bf16[1280,512]{1,0:T(8,128)(2,1)S(1)} %pad_maximum_fusion.1.refs_6_.refs_4_), channel_id=1, source_target_pairs={{0,4},{4,0},{8,12},{12,8},{16,20},{20,16},{24,28},{28,24},{1,5},{5... | collective-permute-start | bytes 3932168 | tf_op jit(solution)/shard_map/ppermute | solution.py:1291
  (41 other events, 198.8 us)
where the time goes:
time: 306 us; the launch traced here: 311 us
  Pallas kernels  118 us (39%)
  starting transfers between devices  96.5 us (32%)
  waiting for transfers between devices  63.5 us (21%)
  local copies, waits for them, and re-layouts  17.4 us (6%)
  other arithmetic  12.4 us (4%)
  between operations  3.38 us (1%)
    pallas_call x11, Pallas kernels, run_kernel(): pl.pallas_call(body, out_shape=[jax.ShapeDtypeStruct(shape, kind) for sha...  118 us
    ppermute x37, starting transfers between devices, swap(): lax.ppermute(block, axis, [(i, i ^ bit) for i in range(lax.axis_size(axis...  77.6 us
    ppermute x37, waiting for transfers between devices, swap(): lax.ppermute(block, axis, [(i, i ^ bit) for i in range(lax.axis_size(axis...  45.8 us
    ppermute x1, waiting for transfers between devices, shards(): lax.ppermute(payload, 'seq', SIDE)  10.6 us
    unnamed x54, local copies, waits for them, and re-layouts  8.4 us
    convert_element_type x23, other arithmetic, bfloat(): return values.astype(bf16)  7.75 us
    ppermute x1, waiting for transfers between devices, shards(): onward = lax.ppermute(middle_part, 'seq', MIDDLE)  6.89 us
  transfers between devices with their start and end apart: 47, of which 16 were waited for; matrix products, arithmetic and copies ran while one was open for 7% of the time, Pallas kernels for 27%

commit v1 on v0

--- a/solution.py
+++ b/solution.py
@@ -469,7 +469,7 @@
     wq, entering, far_k, far_v, far_sum, sums_one, sums_two,
     canvas_out, middle_out, side_out, sent, kept,
     window, tails, codes, keycodes, columns, keys, keys_t, values, grad_keys, grad_values,
-    q_sides, u_sides, fixes, query_t, grad_k, grad_v, semaphores,
+    q_sides, u_sides, fixes, query_t, grad_k, grad_v, late, semaphores,
 ):
     T, D = queries.shape
     place, length = numbers[0], numbers[1]
@@ -512,7 +512,7 @@
     canvas_out[...] = entering[...] + times_transposed(query_rows, wq[...])
     half = kept.shape[0]
     half_side = numbers[3]
-    put_block(bfloat(matmul(jnp.transpose(window[place]), query_rows)), 0, half, half_side, sent, kept)
+    late[0:D, :] = bfloat(matmul(jnp.transpose(window[place]), query_rows))
     inner, beside, across, _ = neighbours(place)
 
     def fold(tile, value_sum):
@@ -540,14 +540,15 @@
 
     value_sum = lax.fori_loop(low, high, fold, far_sum[0:1, :])
     done(0, 1, 2)
-    put_block(bfloat(grad_k[...]), D, half, half_side, sent, kept)
-    put_block(bfloat(grad_v[...]), 2 * D, half, half_side, sent, kept)
+    late[D : 2 * D, :] = bfloat(grad_k[...])
+    late[2 * D : 3 * D, :] = bfloat(grad_v[...])
     vector_sums = jnp.concatenate(
         [sums_one[...], sums_two[...], summed(query_rows), value_sum, jnp.zeros((6, D), f32)], axis=0
     )
-    put_block(bfloat(vector_sums), 3 * D, half, half_side, sent, kept)
-    spare = 2 * half - 3 * D - 32
-    put_block(jnp.zeros((spare, D), bf16), 3 * D + 32, half, half_side, sent, kept)
+    late[3 * D : 3 * D + 32, :] = bfloat(vector_sums)
+    late[3 * D + 32 : 2 * half, :] = jnp.zeros((2 * half - 3 * D - 32, D), bf16)
+    for copy in [ship(late, n * half, half, sent, kept, half_side, semaphores.at[8 + n]) for n in range(2)]:
+        copy.wait()
 
 
 VMEM_BLOCK = pl.BlockSpec(memory_space=pltpu.VMEM)
@@ -569,7 +570,7 @@
         return ref[at]
 
 
-def run_kernel(kernel, name, microseconds, out_shapes, small, far, near, scratch, ties=(), out_far=0):
+def run_kernel(kernel, name, microseconds, out_shapes, small, far, near, scratch, ties=(), out_far=0, anywhere=False):
     kept = out_shapes[: len(out_shapes) - out_far]
     counts = [len(small), len(far), len(near), len(ties), len(kept), out_far, len(scratch), len(near), len(kept), 1]
 
@@ -612,7 +613,8 @@
         body,
         out_shape=[jax.ShapeDtypeStruct(shape, kind) for shape, kind in out_shapes],
         in_specs=[SMEM_BLOCK] * len(small)
-        + [HBM_BLOCK] * (len(far) + len(near))
+        + [HBM_BLOCK] * len(far)
+        + [ANY_BLOCK if anywhere else HBM_BLOCK] * len(near)
         + [ANY_BLOCK] * len(ties),
         out_specs=[HBM_BLOCK] * len(out_shapes),
         scratch_shapes=[
@@ -719,9 +721,10 @@
             pltpu.VMEM((D, T), f32),
             pltpu.VMEM((D, D), f32),
             pltpu.VMEM((D, D), f32),
-            pltpu.SemaphoreType.DMA((8,)),
+            pltpu.VMEM((2 * rows, D), bf16),
+            pltpu.SemaphoreType.DMA((10,)),
         ],
-        ties,
+        ties, 2,
     )
 
 
@@ -854,22 +857,20 @@
         columns[span, :] = as_column(jnp.where(b * here + lane < memory_length, code, -1.0))
 
 
-def put_block(block, start, half, side, sent, kept):
-    size = block.shape[0]
-    for part in range(2):
-        low, high = max(start, part * half), min(start + size, (part + 1) * half)
-        if low >= high:
-            continue
-        rows = block[low - start : high - start]
-        at = slice(low - part * half, high - part * half)
-
-        @pl.when(side == part)
-        def _():
-            kept[at, :] = rows
-
-        @pl.when(side != part)
-        def _():
-            sent[at, :] = rows
+def ship(buffer, first, count, sent, kept, side, semaphore):
+    half = kept.shape[0]
+    part, at = divmod(first, half)
+    source = buffer.at[pl.ds(first, count)]
+
+    @pl.when(side == part)
+    def _():
+        pltpu.make_async_copy(source, kept.at[pl.ds(at, count)], semaphore).start()
+
+    @pl.when(side != part)
+    def _():
+        pltpu.make_async_copy(source, sent.at[pl.ds(at, count)], semaphore).start()
+
+    return pltpu.make_async_copy(source, kept.at[pl.ds(at, count)], semaphore)
 
 
 def forward_kernel(
@@ -896,24 +897,14 @@
         copy.start()
     leaving = []
 
-    half = sent.shape[0]
     half_side = numbers[3]
 
     def leave(block, index):
         early[pl.ds(index * D, D), :] = block
-        part, start_row = divmod(index * D, half)
-        source = early.at[pl.ds(index * D, D)]
-        rows = pl.ds(start_row, D)
-
-        @pl.when(half_side == part)
-        def _():
-            pltpu.make_async_copy(source, kept.at[rows], semaphores.at[6 + index]).start()
-
-        @pl.when(half_side != part)
-        def _():
-            pltpu.make_async_copy(source, sent.at[rows], semaphores.at[6 + index]).start()
-
-        leaving.append(pltpu.make_async_copy(source, kept.at[rows], semaphores.at[6 + index]))
+
+    def go(*indices):
+        for index in indices:
+            leaving.append(ship(early, index * D, D, sent, kept, half_side, semaphores.at[6 + index]))
 
     def vector(index):
         return vectors[index : index + 1, :]
@@ -1045,9 +1036,13 @@
         leave(bfloat(matmul(low2_t, before_grad)), 2 + c)
         sums[4 + c : 5 + c, :] = summed(before_grad)
         second_up += times_transposed(before_grad, we[:, lanes])
+        if c == FF // D // 2:
+            go(0, 1, *[2 + n for n in range(c)], *[2 + FF // D + n for n in range(c)])
     second_out[...] = norm_backward(second_up, vector(G2), normal2, scaling2)
     sums[8:9, :] = summed(second_up * normal2)
     sums[9:10, :] = summed(second_up)
+    rest = range(FF // D // 2, FF // D)
+    go(*[2 + n for n in rest], *[2 + FF // D + n for n in rest])
     for copy in leaving:
         copy.wait()
 
@@ -1056,8 +1051,8 @@
     ready, done, numbers,
     second_grad, co, segments, vectors, gathered, query, ck, cv, fetched, lse, cq, normal, scaling, wo, low,
     blended, first_state, wv, self_lse,
-    first_grad_out, upstream_out, memory_out, sent, kept, sums,
-    memory, columns, keys, keys_t, values, grad_keys, grad_values, query_t, upstream2, q_sides, u_sides, fixes,
+    first_grad_out, upstream_out, sums, sent, kept, memory_goes, memory_stays,
+    memory, columns, keys, keys_t, values, grad_keys, grad_values, query_t, upstream2, q_sides, u_sides, fixes, late, memory_out, semaphores,
 ):
     T, D = low.shape
     M = memory.shape[0]
@@ -1110,20 +1105,39 @@
             jnp.logical_and(tail == 1, jnp.logical_and(is_outer(place), place == 3 - b)), opposite_row, 0.0
         )
         memory_out[b, here:size, :] = bfloat(rows)
-    done(2)
+    leaving = []
+    for b in range(count):
+        copies = [
+            pltpu.make_async_copy(memory_out.at[b], half_out.at[b // 2], semaphores.at[2 + b])
+            for half_out in (memory_stays, memory_goes)
+        ]
+
+        @pl.when(lax.rem(place, 2) == b % 2)
+        def _():
+            copies[0].start()
+
+        @pl.when(lax.rem(place, 2) != b % 2)
+        def _():
+            copies[1].start()
+
+        leaving.append(copies[0])
+    memory_t = jnp.transpose(memory[...])
+    late[0:D, :] = bfloat(matmul(jnp.transpose(low[...]), query_rows))
+    late[D : 2 * D, :] = bfloat(matmul(memory_t, gk))
+    late[2 * D : 3 * D, :] = bfloat(matmul(memory_t, gv))
+    late[3 * D : 4 * D, :] = bfloat(matmul(jnp.transpose(fetched[...]), low_grad))
+    late[4 * D : 5 * D, :] = bfloat(matmul(jnp.transpose(blended[...]), first_low))
     half = 5 * D // 2
-    memory_t = jnp.transpose(memory[...])
-    put_block(bfloat(matmul(jnp.transpose(low[...]), query_rows)), 0, half, half_side, sent, kept)
-    put_block(bfloat(matmul(memory_t, gk)), D, half, half_side, sent, kept)
-    put_block(bfloat(matmul(memory_t, gv)), 2 * D, half, half_side, sent, kept)
-    put_block(bfloat(matmul(jnp.transpose(fetched[...]), low_grad)), 3 * D, half, half_side, sent, kept)
-    put_block(bfloat(matmul(jnp.transpose(blended[...]), first_low)), 4 * D, half, half_side, sent, kept)
+    leaving += [ship(late, n * half, half, sent, kept, half_side, semaphores.at[n]) for n in range(2)]
     sums[0:1, :] = summed(low_grad)
     sums[1:2, :] = summed(query_rows)
     sums[2:3, :] = summed(gv)
     sums[3:4, :] = summed(first_up * normal[...])
     sums[4:5, :] = summed(first_up)
     sums[5:6, :] = summed(first_low)
+    done(2)
+    for copy in leaving:
+        copy.wait()
 
 
 def middle_forward(numbers, segments, canvas, blended, cotangent, vectors, blocks, last_memory, weights, ties=()):
@@ -1167,13 +1181,14 @@
     T, D = blended.shape
     M = gathered.shape[0] * (gathered.shape[1] - TAIL)
     rows = 5 * D // 2
+    part = (gathered.shape[0] // 2, *gathered.shape[1:])
     normal, scaling, low, query, fetched, lse, second_grad, first_state, self_lse = saved
     wo, cq, ck, cv, co, wv = weights
     return run_kernel(
         backward_kernel, "middle_backward", 16,
         [
-            ((T, D), f32), ((T, D), bf16), (gathered.shape, bf16),
-            ((rows, D), bf16), ((rows, D), bf16), ((8, D), f32),
+            ((T, D), f32), ((T, D), bf16), ((8, D), f32), ((rows, D), bf16), ((rows, D), bf16),
+            (part, bf16), (part, bf16),
         ],
         numbers, [],
         [
@@ -1193,8 +1208,11 @@
             pltpu.VMEM((H, T, 128), bf16),
             pltpu.VMEM((H, T, 128), bf16),
             pltpu.VMEM((H, T), f32),
+            pltpu.VMEM((2 * rows, D), bf16),
+            pltpu.VMEM(gathered.shape, bf16),
+            pltpu.SemaphoreType.DMA((6,)),
         ],
-        ties,
+        ties, 4,
     )
 
 
@@ -1238,7 +1256,7 @@
     return run_kernel(
         functools.partial(unpack_kernel, [starts for _, starts in layout]), name, 4,
         [((count, D * len(starts)), f32) for count, starts in layout],
-        numbers, [], [mine, came], [], ties,
+        numbers, [], [mine, came], [], ties, 0, True,
     )
 
 
@@ -1487,7 +1505,7 @@
     order = Order()
     early = Summing(order, early_sent, early_kept, 2)
     early.step()
-    first_grad, blended_grad, memory_part, later_sent, later_kept, later_sums = middle_backward(
+    first_grad, blended_grad, later_sums, later_sent, later_kept, memory_goes, memory_stays = middle_backward(
         numbers, canvas_segments, blended, gathered, vectors,
         (normal, scaling, low, cross_rows, fetched, cross_masses, second_grad, first_state, masses),
         (self_output, cross_query, cross_key, cross_value, cross_output, self_value), order.last,
@@ -1503,7 +1521,6 @@
     from_side = lax.ppermute(far_part, "seq", INWARD)
     from_middle = lax.ppermute(far_part, "seq", MIDDLE)
     near_step, far_step = routes()[3]
-    memory_goes, memory_stays = entry_halves(memory_part, near_step, 1)
     memory_came = swap(memory_goes, near_step)
     early.step()
     (memory_came,) = order.after(memory_came)

time: 306 us -> 316 us (1.033); the launches traced: 311 us -> 310 us
  Pallas kernels: 118 us -> 111 us
  waiting for transfers between devices: 63.5 us -> 69.6 us
    pallas_call x11, Pallas kernels: 118 us -> 111 us  [run_kernel(): pl.pallas_call(body, out_shape=[jax.ShapeDtypeStruct(shape, kind) for sha...]
    ppermute x37, waiting for transfers between devices: 45.8 us -> 52.2 us  [swap(): lax.ppermute(block, axis, [(i, i ^ bit) for i in range(lax.axis_size(axis...]
  transfers between devices with their start and end apart: 47 -> 47, of which waited for: 16 -> 16; matrix products, arithmetic and copies ran while one was open for 7% -> 6% of each run, Pallas kernels for 27% -> 25%
where the time goes in v1:
time: 316 us; the launch traced here: 310 us
  Pallas kernels  111 us (35%)
  starting transfers between devices  98.2 us (31%)
  waiting for transfers between devices  69.6 us (22%)
  local copies, waits for them, and re-layouts  15.7 us (5%)
  other arithmetic  12.4 us (4%)
  between operations  3.45 us (1%)
    pallas_call x11, Pallas kernels, run_kernel(): pl.pallas_call(body, out_shape=[jax.ShapeDtypeStruct(shape, kind) for sha...  111 us
    ppermute x37, starting transfers between devices, swap(): lax.ppermute(block, axis, [(i, i ^ bit) for i in range(lax.axis_size(axis...  80.6 us
    ppermute x37, waiting for transfers between devices, swap(): lax.ppermute(block, axis, [(i, i ^ bit) for i in range(lax.axis_size(axis...  52.2 us
    ppermute x1, waiting for transfers between devices, shards(): lax.ppermute(payload, 'seq', SIDE)  10.6 us
    unnamed x54, local copies, waits for them, and re-layouts  8.37 us
    convert_element_type x23, other arithmetic, bfloat(): return values.astype(bf16)  7.78 us
    ppermute x1, waiting for transfers between devices, shards(): onward = lax.ppermute(middle_part, 'seq', MIDDLE)  6.63 us
  transfers between devices with their start and end apart: 47, of which 16 were waited for; matrix products, arithmetic and copies ran while one was open for 6% of the time, Pallas kernels for 25%

profile of v1, /device:TPU:9, one launch (start us, length us, event | category | flops | bytes accessed | tf_op | source)
XLA Modules:
  0.0 310.4 jit_solution(2350681283920347053)
XLA Ops:
  2.6 3.6 %pack.1 = (f32[18,512]{1,0:T(8,128)}, bf16[672,512]{1,0:T(8,128)(2,1)}) custom-call(s32[2]{0:T(128)} %pad_add_fusion.refs_0_, s32[1]{0:T(128)S(6)} %copy.63.refs_1_, s32[1]{0:T(128)S(6)} %copy.64.refs_2_, s32[1,512]{1,0:T(1,128)} %refs_3_.21, bf16[512,512]{1,0:T(8,128)(2,1)} %bitcast.43, bf16[512,512]{1,0:T(8,128)(2,1)} %bitcast.45, bf16[512]{0:T(512)(128)(2,1)} %refs_6_.3, ...), custom_call_target="tpu_custom_call" | custom-call | flops 2200000000 | tf_op jit(solution)/shard_map/pack/pallas_call | solution.py:612
  6.3 4.5 %collective-permute-start.1 = (bf16[672,512]{1,0:T(8,128)(2,1)}, bf16[672,512]{1,0:T(8,128)(2,1)S(1)}, u32[]{:S(2)}, u32[]{:S(2)}) collective-permute-start(bf16[672,512]{1,0:T(8,128)(2,1)} %get-tuple-element.116.refs_4_), channel_id=1, source_target_pairs={{1,2},{2,1},{5,6},{6,5},{9,10},{10,9},{13,14},{14,13},{17,18},{18,... | collective-permute-start | bytes 2064392 | tf_op jit(solution)/shard_map/ppermute | solution.py:1486
  12.1 10.6 %collective-permute-done.refs_5_ = bf16[672,512]{1,0:T(8,128)(2,1)S(1)} collective-permute-done((bf16[672,512]{1,0:T(8,128)(2,1)}, bf16[672,512]{1,0:T(8,128)(2,1)S(1)}, u32[]{:S(2)}, u32[]{:S(2)}) %collective-permute-start) | collective-permute-done | bytes 688160 | tf_op jit(solution)/shard_map/ppermute | solution.py:1486
  22.8 3.2 %collective-permute-start.2 = (bf16[672,512]{1,0:T(8,128)(2,1)S(1)}, bf16[672,512]{1,0:T(8,128)(2,1)S(1)}, u32[]{:S(2)}, u32[]{:S(2)}) collective-permute-start(bf16[672,512]{1,0:T(8,128)(2,1)S(1)} %collective-permute-done.refs_5_), channel_id=1, source_target_pairs={{1,2},{2,1},{5,6},{6,5},{9,10},{10,9},{13,14},{14,13},{17,18},{18,... | collective-permute-start | bytes 2064392 | tf_op jit(solution)/shard_map/ppermute | solution.py:1489
  27.5 13.1 %self_near.1 = (bf16[512,512]{1,0:T(8,128)(2,1)}, f32[8,80,512]{2,1,0:T(8,128)}, f32[16,128]{1,0:T(8,128)}) custom-call(s32[2]{0:T(128)} %pad_add_fusion.refs_0_, s32[1]{0:T(128)S(6)} %copy.63.refs_1_, s32[1]{0:T(128)S(6)} %copy.64.refs_2_, s32[1,512]{1,0:T(1,128)} %refs_3_.21, bf16[672,512]{1,0:T(8,128)(2,1)} %get-tuple-element.116.refs_4_, ...), custom_call_target="tpu_custom_call" | custom-call | flops 14300000256 | tf_op jit(solution)/shard_map/self_near/pallas_call | solution.py:612
  42.8 4.7 %self_far.1 = (bf16[512,512]{1,0:T(8,128)(2,1)}, f32[8,512]{1,0:T(8,128)}) custom-call(s32[2]{0:T(128)} %pad_add_fusion.refs_0_, s32[1]{0:T(128)S(6)} %copy.63.refs_1_, s32[1]{0:T(128)S(6)} %copy.64.refs_2_, s32[1,512]{1,0:T(1,128)} %refs_3_.21, bf16[672,512]{1,0:T(8,128)(2,1)} %get-tuple-element.116.refs_4_, bf16[672,512]{1,0:T(8,128)(2,1)} %copy-done.18, ...), custom_call_target="tpu_custom_call" | custom-call | flops 7699999744 | tf_op jit(solution)/shard_map/self_far/pallas_call | solution.py:612
  48.2 26.3 %middle_forward.1 = (bf16[512,512]{1,0:T(8,128)(2,1)}, f32[8,512]{1,0:T(8,128)}, bf16[16,512]{1,0:T(8,128)(2,1)}, f32[512,512]{1,0:T(8,128)}, f32[512,128]{1,0:T...) custom-call(s32[2]{0:T(128)} %pad_add_fusion.refs_0_, ...), custom_call_target="tpu_custom_call" | custom-call | flops 26400000000 | tf_op jit(solution)/shard_map/middle_forward/pallas_call | solution.py:612
  74.5 4.7 %collective-permute-start.6 = (bf16[2560,512]{1,0:T(8,128)(2,1)}, bf16[2560,512]{1,0:T(8,128)(2,1)S(1)}, u32[]{:S(2)}, u32[]{:S(2)}) collective-permute-start(bf16[2560,512]{1,0:T(8,128)(2,1)} %get-tuple-element.133), channel_id=1, source_target_pairs={{0,4},{4,0},{8,12},{12,8},{16,20},{20,16},{24,28},{28,24},{1,5},{5... | collective-permute-start | bytes 7864328 | tf_op jit(solution)/shard_map/ppermute | solution.py:1309
  81.0 2.9 collective-permute-done.6
  84.5 34.2 %collective-permute-start.8 = (bf16[640,512]{1,0:T(8,128)(2,1)S(1)}, bf16[640,512]{1,0:T(8,128)(2,1)S(1)}, u32[]{:S(2)}, u32[]{:S(2)}) collective-permute-start(bf16[640,512]{1,0:T(8,128)(2,1)S(1)} %get-tuple-element.208.refs_23_), channel_id=1, source_target_pairs={{0,8},{4,12},{8,0},{12,4},{16,24},{20,28},{24,16},{28,20},{1,9},{5... | collective-permute-start | bytes 1966088 | tf_op jit(solution)/shard_map/ppermute | solution.py:1309
  119.9 17.0 %middle_backward.1 = (f32[512,512]{1,0:T(8,128)}, bf16[512,512]{1,0:T(8,128)(2,1)}, f32[8,512]{1,0:T(8,128)}, bf16[1280,512]{1,0:T(8,128)(2,1)}, bf16[1280,512]{...) custom-call(s32[2]{0:T(128)} %pad_add_fusion.refs_0_, s32[1]{0:T(128)S(6)} %copy.63.refs_1_, ...), custom_call_target="tpu_custom_call" | custom-call | flops 17600000000 | tf_op jit(solution)/shard_map/middle_backward/pallas_call | solution.py:612
  139.8 4.9 %back_far.1 = (bf16[512,512]{1,0:T(8,128)(2,1)}, f32[512,512]{1,0:T(8,128)}, f32[512,512]{1,0:T(8,128)}, f32[8,512]{1,0:T(8,128)}, f32[512,512]{1,0:T(8,128)}) custom-call(s32[2]{0:T(128)} %pad_add_fusion.refs_0_, s32[1]{0:T(128)S(6)} %copy.63.refs_1_, s32[1]{0:T(128)S(6)} %copy.64.refs_2_, s32[1,512]{1,0:T(1,128)} %refs_3_.21, bf16[672,512]{1,0:T(8,128)(2,1)} %copy-done.15, ...), custom_call_target="tpu_custom_call" | custom-call | flops 8800000000 | tf_op jit(solution)/shard_map/back_far/pallas_call | solution.py:612
  147.3 2.6 collective-permute-start.15
  153.0 4.5 %collective-permute-start.16 = (bf16[640,512]{1,0:T(8,128)(2,1)S(1)}, bf16[640,512]{1,0:T(8,128)(2,1)S(1)}, u32[]{:S(2)}, u32[]{:S(2)}) collective-permute-start(bf16[640,512]{1,0:T(8,128)(2,1)S(1)} %get-tuple-element.204.refs_23_), channel_id=1, source_target_pairs={{0,8},{4,12},{8,0},{12,4},{16,24},{20,28},{24,16},{28,20},{1,9},{5... | collective-permute-start | bytes 1966088 | tf_op jit(solution)/shard_map/ppermute | solution.py:1309
  157.5 21.4 %back_near.1 = (f32[512,512]{1,0:T(8,128)}, bf16[512,512]{1,0:T(8,128)(2,1)}, bf16[512,512]{1,0:T(8,128)(2,1)}, bf16[896,512]{1,0:T(8,128)(2,1)}, bf16[896,512]{1,0:T(8,128)(2,1)}) custom-call(s32[2]{0:T(128)} %pad_add_fusion.refs_0_, s32[1]{0:T(128)S(6)} %copy.63.refs_1_, s32[1]{0:T(128)S(6)} %copy.64.refs_2_, s32[1,512]{1,0:T(1,128)} %refs_3_.21, ...), custom_call_target="tpu_custom_call" | custom-call | flops 24199999488 | tf_op jit(solution)/shard_map/back_near/pallas_call | solution.py:612
  178.8 6.0 %collective-permute-start.21 = (bf16[896,512]{1,0:T(8,128)(2,1)}, bf16[896,512]{1,0:T(8,128)(2,1)S(1)}, u32[]{:S(2)}, u32[]{:S(2)}) collective-permute-start(bf16[896,512]{1,0:T(8,128)(2,1)} %get-tuple-element.157), channel_id=1, source_target_pairs={{0,4},{4,0},{8,12},{12,8},{16,20},{20,16},{24,28},{28,24},{1,5},{5... | collective-permute-start | bytes 2752520 | tf_op jit(solution)/shard_map/ppermute | solution.py:1309
  186.4 7.5 %collective-permute-start.20 = (bf16[320,512]{1,0:T(8,128)(2,1)S(1)}, bf16[320,512]{1,0:T(8,128)(2,1)}, u32[]{:S(2)}, u32[]{:S(2)}) collective-permute-start(bf16[320,512]{1,0:T(8,128)(2,1)S(1)} %get-tuple-element.220), channel_id=1, source_target_pairs={{0,16},{4,20},{8,24},{12,28},{16,0},{20,4},{24,8},{28,12},{1,17},{... | collective-permute-start | bytes 983048 | tf_op jit(solution)/shard_map/ppermute | solution.py:1309
  195.4 6.2 %collective-permute-done.20 = bf16[320,512]{1,0:T(8,128)(2,1)} collective-permute-done((bf16[320,512]{1,0:T(8,128)(2,1)S(1)}, bf16[320,512]{1,0:T(8,128)(2,1)}, u32[]{:S(2)}, u32[]{:S(2)}) %collective-permute-start.20) | collective-permute-done | bytes 327712 | tf_op jit(solution)/shard_map/ppermute | solution.py:1309
  202.7 3.9 %collective-permute-done.25 = bf16[224,512]{1,0:T(8,128)(2,1)} collective-permute-done((bf16[224,512]{1,0:T(8,128)(2,1)S(1)}, bf16[224,512]{1,0:T(8,128)(2,1)}, u32[]{:S(2)}, u32[]{:S(2)}) %collective-permute-start.25) | collective-permute-done | bytes 229408 | tf_op jit(solution)/shard_map/ppermute | solution.py:1309
  210.0 4.4 %collective-permute-start.30 = (bf16[320,512]{1,0:T(8,128)(2,1)S(1)}, bf16[320,512]{1,0:T(8,128)(2,1)S(1)}, u32[]{:S(2)}, u32[]{:S(2)}) collective-permute-start(bf16[320,512]{1,0:T(8,128)(2,1)S(1)} %add_convert_fusion.8), channel_id=1, source_target_pairs={{0,1},{1,0},{2,3},{3,2},{4,5},{5,4},{6,7},{7,6},{8,9},{9,8},{10,11... | collective-permute-start | bytes 983048 | tf_op jit(solution)/shard_map/ppermute | solution.py:1309
  215.7 8.7 %collective-permute-done.30 = bf16[320,512]{1,0:T(8,128)(2,1)S(1)} collective-permute-done((bf16[320,512]{1,0:T(8,128)(2,1)S(1)}, bf16[320,512]{1,0:T(8,128)(2,1)S(1)}, u32[]{:S(2)}, u32[]{:S(2)}) %collective-permute-start.30) | collective-permute-done | bytes 327712 | tf_op jit(solution)/shard_map/ppermute | solution.py:1309
  225.5 2.4 collective-permute-done.29
  234.8 2.3 collective-permute-start.36
  239.4 12.1 %collective-permute-done.39 = bf16[640,512]{1,0:T(8,128)(2,1)S(1)} collective-permute-done((bf16[640,512]{1,0:T(8,128)(2,1)S(1)}, bf16[640,512]{1,0:T(8,128)(2,1)S(1)}, u32[]{:S(2)}, u32[]{:S(2)}) %collective-permute-start.39) | collective-permute-done | bytes 655392 | tf_op jit(solution)/shard_map/ppermute | solution.py:1309
  252.3 2.8 collective-permute-start.43
  258.9 2.6 collective-permute-start.18
  262.4 7.3 %collective-permute-done.34 = bf16[320,512]{1,0:T(8,128)(2,1)S(1)} collective-permute-done((bf16[320,512]{1,0:T(8,128)(2,1)S(1)}, bf16[320,512]{1,0:T(8,128)(2,1)S(1)}, u32[]{:S(2)}, u32[]{:S(2)}) %collective-permute-start.34) | collective-permute-done | bytes 327712 | tf_op jit(solution)/shard_map/ppermute | solution.py:1309
  270.8 6.6 %collective-permute-done.18.refs_10_ = bf16[512,512]{1,0:T(8,128)(2,1)S(1)} collective-permute-done((bf16[512,512]{1,0:T(8,128)(2,1)S(1)}, bf16[512,512]{1,0:T(8,128)(2,1)S(1)}, u32[]{:S(2)}, u32[]{:S(2)}) %collective-permute-start.18) | collective-permute-done | bytes 524320 | tf_op jit(solution)/shard_map/ppermute | solution.py:1547
  279.0 3.9 %finish.1 = (f32[128,512]{1,0:T(8,128)}, bf16[512,512]{1,0:T(8,128)(2,1)}, f32[512,512]{1,0:T(8,128)}) custom-call(s32[2]{0:T(128)} %pad_add_fusion.refs_0_, s32[1]{0:T(128)S(6)} %copy.63.refs_1_, s32[1]{0:T(128)S(6)} %copy.64.refs_2_, s32[1,512]{1,0:T(1,128)} %refs_3_.21, bf16[144,512]{1,0:T(8,128)(2,1)} %get-tuple-element.260.refs_4_, ...), custom_call_target="tpu_custom_call" | custom-call | flops 3300000000 | tf_op jit(solution)/shard_map/finish/pallas_call | solution.py:612
  282.9 7.5 %early_out.1 = (f32[1024,512]{1,0:T(8,128)}, f32[512,2048]{1,0:T(8,128)}, f32[2048,512]{1,0:T(8,128)}) custom-call(s32[2]{0:T(128)} %pad_add_fusion.refs_0_, s32[1]{0:T(128)S(6)} %copy.63.refs_1_, s32[1]{0:T(128)S(6)} %copy.64.refs_2_, s32[1,512]{1,0:T(1,128)} %refs_3_.21, bf16[2560,512]{1,0:T(8,128)(2,1)} %copy-done, ...), custom_call_target="tpu_custom_call" | custom-call | flops 4400000000 | tf_op jit(solution)/shard_map/early_out/pallas_call | solution.py:612
  297.1 3.9 %last_out.1 = (f32[512,512]{1,0:T(8,128)}, f32[512,512]{1,0:T(8,128)}, f32[512,512]{1,0:T(8,128)}, f32[32,512]{1,0:T(8,128)}) custom-call(s32[2]{0:T(128)} %pad_add_fusion.refs_0_, s32[1]{0:T(128)S(6)} %copy.63.refs_1_, s32[1]{0:T(128)S(6)} %copy.64.refs_2_, s32[1,512]{1,0:T(1,128)} %refs_3_.21, bf16[896,512]{1,0:T(8,128)(2,1)} %copy-done.3, ...), custom_call_target="tpu_custom_call" | custom-call | flops 4400000000 | tf_op jit(solution)/shard_map/last_out/pallas_call | solution.py:612
  305.0 4.9 %later_out.1 = (f32[512,512]{1,0:T(8,128)}, f32[512,512]{1,0:T(8,128)}, f32[512,512]{1,0:T(8,128)}, f32[512,512]{1,0:T(8,128)}, f32[512,512]{1,0:T(8,128)}) custom-call(s32[2]{0:T(128)} %pad_add_fusion.refs_0_, s32[1]{0:T(128)S(6)} %copy.63.refs_1_, s32[1]{0:T(128)S(6)} %copy.64.refs_2_, s32[1,512]{1,0:T(1,128)} %refs_3_.21, bf16[1280,512]{1,0:T(8,128)(2,1)} %copy-done.2, ...), custom_call_target="tpu_custom_call" | custom-call | flops 4400000000 | tf_op jit(solution)/shard_map/later_out/pallas_call | solution.py:612
  (192 shorter events, 55.9 us)
Async XLA Ops:
  6.2 16.6 %collective-permute-start = (bf16[672,512]{1,0:T(8,128)(2,1)}, bf16[672,512]{1,0:T(8,128)(2,1)S(1)}, u32[]{:S(2)}, u32[]{:S(2)}) collective-permute-start(bf16[672,512]{1,0:T(8,128)(2,1)} %get-tuple-element.116.refs_4_), channel_id=1, source_target_pairs={{0,1},{1,0},{2,3},{3,2},{4,5},{5,4},{6,7},{7,6},{8,9},{9,8},{10,11... | collective-permute-start | bytes 2064392 | tf_op jit(solution)/shard_map/ppermute | solution.py:1486
  6.3 19.9 %collective-permute-start.1 = (bf16[672,512]{1,0:T(8,128)(2,1)}, bf16[672,512]{1,0:T(8,128)(2,1)S(1)}, u32[]{:S(2)}, u32[]{:S(2)}) collective-permute-start(bf16[672,512]{1,0:T(8,128)(2,1)} %get-tuple-element.116.refs_4_), channel_id=1, source_target_pairs={{1,2},{2,1},{5,6},{6,5},{9,10},{10,9},{13,14},{14,13},{17,18},{18,... | collective-permute-start | bytes 2064392 | tf_op jit(solution)/shard_map/ppermute | solution.py:1486
  11.5 30.5 %collective-permute-start.5 = (bf16[16,512]{1,0:T(8,128)(2,1)S(1)}, bf16[16,512]{1,0:T(8,128)(2,1)S(1)}, u32[]{:S(2)}, u32[]{:S(2)}) collective-permute-start(bf16[16,512]{1,0:T(8,128)(2,1)S(1)} %slice.103), channel_id=1, source_target_pairs={{0,3},{3,0},{4,7},{7,4},{8,11},{11,8},{12,15},{15,12},{16,19},{19,... | collective-permute-start | bytes 49160 | tf_op jit(solution)/shard_map/ppermute | solution.py:1487
  22.8 17.8 %collective-permute-start.2 = (bf16[672,512]{1,0:T(8,128)(2,1)S(1)}, bf16[672,512]{1,0:T(8,128)(2,1)S(1)}, u32[]{:S(2)}, u32[]{:S(2)}) collective-permute-start(bf16[672,512]{1,0:T(8,128)(2,1)S(1)} %collective-permute-done.refs_5_), channel_id=1, source_target_pairs={{1,2},{2,1},{5,6},{6,5},{9,10},{10,9},{13,14},{14,13},{17,18},{18,... | collective-permute-start | bytes 2064392 | tf_op jit(solution)/shard_map/ppermute | solution.py:1489
  26.1 15.8 %collective-permute-start.3 = (bf16[672,512]{1,0:T(8,128)(2,1)S(1)}, bf16[672,512]{1,0:T(8,128)(2,1)S(1)}, u32[]{:S(2)}, u32[]{:S(2)}) collective-permute-start(bf16[672,512]{1,0:T(8,128)(2,1)S(1)} %collective-permute-done.1.refs_6_), channel_id=1, source_target_pairs={{1,0},{2,3},{5,4},{6,7},{9,8},{10,11},{13,12},{14,15},{17,16},{18,... | collective-permute-start | bytes 2064392 | tf_op jit(solution)/shard_map/ppermute | solution.py:1489
  84.5 53.2 %collective-permute-start.8 = (bf16[640,512]{1,0:T(8,128)(2,1)S(1)}, bf16[640,512]{1,0:T(8,128)(2,1)S(1)}, u32[]{:S(2)}, u32[]{:S(2)}) collective-permute-start(bf16[640,512]{1,0:T(8,128)(2,1)S(1)} %get-tuple-element.208.refs_23_), channel_id=1, source_target_pairs={{0,8},{4,12},{8,0},{12,4},{16,24},{20,28},{24,16},{28,20},{1,9},{5... | collective-permute-start | bytes 1966088 | tf_op jit(solution)/shard_map/ppermute | solution.py:1309
  119.1 18.6 %collective-permute-start.9 = (bf16[640,512]{1,0:T(8,128)(2,1)S(1)}, bf16[640,512]{1,0:T(8,128)(2,1)S(1)}, u32[]{:S(2)}, u32[]{:S(2)}) collective-permute-start(bf16[640,512]{1,0:T(8,128)(2,1)S(1)} %get-tuple-element.206.refs_24_), channel_id=1, source_target_pairs={{0,16},{4,20},{8,24},{12,28},{16,0},{20,4},{24,8},{28,12},{1,17},{... | collective-permute-start | bytes 1966088 | tf_op jit(solution)/shard_map/ppermute | solution.py:1309
  136.9 13.3 %collective-permute-start.7 = (bf16[2,144,512]{2,1,0:T(8,128)(2,1)}, bf16[2,144,512]{2,1,0:T(8,128)(2,1)}, u32[]{:S(2)}, u32[]{:S(2)}) collective-permute-start(bf16[2,144,512]{2,1,0:T(8,128)(2,1)} %get-tuple-element.135), channel_id=1, source_target_pairs={{0,1},{1,0},{2,3},{3,2},{4,5},{5,4},{6,7},{7,6},{8,9},{9,8},{10,11... | collective-permute-start | bytes 884744 | tf_op jit(solution)/shard_map/ppermute | solution.py:1309
  137.0 15.6 %collective-permute-start.13 = (bf16[1280,512]{1,0:T(8,128)(2,1)}, bf16[1280,512]{1,0:T(8,128)(2,1)S(1)}, u32[]{:S(2)}, u32[]{:S(2)}) collective-permute-start(bf16[1280,512]{1,0:T(8,128)(2,1)} %get-tuple-element.152), channel_id=1, source_target_pairs={{0,4},{4,0},{8,12},{12,8},{16,20},{20,16},{24,28},{28,24},{1,5},{5... | collective-permute-start | bytes 3932168 | tf_op jit(solution)/shard_map/ppermute | solution.py:1309
  139.1 10.7 %collective-permute-start.11 = (bf16[320,512]{1,0:T(8,128)(2,1)S(1)}, bf16[320,512]{1,0:T(8,128)(2,1)S(1)}, u32[]{:S(2)}, u32[]{:S(2)}) collective-permute-start(bf16[320,512]{1,0:T(8,128)(2,1)S(1)} %get-tuple-element.224.refs_16_), channel_id=1, source_target_pairs={{0,8},{4,12},{8,0},{12,4},{16,24},{20,28},{24,16},{28,20},{1,9},{5... | collective-permute-start | bytes 983048 | tf_op jit(solution)/shard_map/ppermute | solution.py:1309
  144.7 49.2 %collective-permute-start.14 = (bf16[512,512]{1,0:T(8,128)(2,1)}, bf16[512,512]{1,0:T(8,128)(2,1)S(1)}, u32[]{:S(2)}, u32[]{:S(2)}) collective-permute-start(bf16[512,512]{1,0:T(8,128)(2,1)} %get-tuple-element.156), channel_id=1, source_target_pairs={{0,1},{3,2},{4,5},{7,6},{8,9},{11,10},{12,13},{15,14},{16,17},{19,... | collective-permute-start | bytes 1572872 | tf_op jit(solution)/shard_map/ppermute | solution.py:1521
  147.3 46.7 %collective-permute-start.15 = (bf16[512,512]{1,0:T(8,128)(2,1)}, bf16[512,512]{1,0:T(8,128)(2,1)S(1)}, u32[]{:S(2)}, u32[]{:S(2)}) collective-permute-start(bf16[512,512]{1,0:T(8,128)(2,1)} %get-tuple-element.156), channel_id=1, source_target_pairs={{1,2},{2,1},{5,6},{6,5},{9,10},{10,9},{13,14},{14,13},{17,18},{18,... | collective-permute-start | bytes 1572872 | tf_op jit(solution)/shard_map/ppermute | solution.py:1522
  150.1 36.0 %collective-permute-start.17 = (bf16[320,512]{1,0:T(8,128)(2,1)S(1)}, bf16[320,512]{1,0:T(8,128)(2,1)S(1)}, u32[]{:S(2)}, u32[]{:S(2)}) collective-permute-start(bf16[320,512]{1,0:T(8,128)(2,1)S(1)} %pad_maximum_fusion.6), channel_id=1, source_target_pairs={{0,1},{1,0},{2,3},{3,2},{4,5},{5,4},{6,7},{7,6},{8,9},{9,8},{10,11... | collective-permute-start | bytes 983048 | tf_op jit(solution)/shard_map/ppermute | solution.py:1309
  153.0 33.2 %collective-permute-start.16 = (bf16[640,512]{1,0:T(8,128)(2,1)S(1)}, bf16[640,512]{1,0:T(8,128)(2,1)S(1)}, u32[]{:S(2)}, u32[]{:S(2)}) collective-permute-start(bf16[640,512]{1,0:T(8,128)(2,1)S(1)} %get-tuple-element.204.refs_23_), channel_id=1, source_target_pairs={{0,8},{4,12},{8,0},{12,4},{16,24},{20,28},{24,16},{28,20},{1,9},{5... | collective-permute-start | bytes 1966088 | tf_op jit(solution)/shard_map/ppermute | solution.py:1309
  178.8 15.4 %collective-permute-start.21 = (bf16[896,512]{1,0:T(8,128)(2,1)}, bf16[896,512]{1,0:T(8,128)(2,1)S(1)}, u32[]{:S(2)}, u32[]{:S(2)}) collective-permute-start(bf16[896,512]{1,0:T(8,128)(2,1)} %get-tuple-element.157), channel_id=1, source_target_pairs={{0,4},{4,0},{8,12},{12,8},{16,20},{20,16},{24,28},{28,24},{1,5},{5... | collective-permute-start | bytes 2752520 | tf_op jit(solution)/shard_map/ppermute | solution.py:1309
  186.4 15.3 %collective-permute-start.20 = (bf16[320,512]{1,0:T(8,128)(2,1)S(1)}, bf16[320,512]{1,0:T(8,128)(2,1)}, u32[]{:S(2)}, u32[]{:S(2)}) collective-permute-start(bf16[320,512]{1,0:T(8,128)(2,1)S(1)} %get-tuple-element.220), channel_id=1, source_target_pairs={{0,16},{4,20},{8,24},{12,28},{16,0},{20,4},{24,8},{28,12},{1,17},{... | collective-permute-start | bytes 983048 | tf_op jit(solution)/shard_map/ppermute | solution.py:1309
  194.6 11.9 %collective-permute-start.25 = (bf16[224,512]{1,0:T(8,128)(2,1)S(1)}, bf16[224,512]{1,0:T(8,128)(2,1)}, u32[]{:S(2)}, u32[]{:S(2)}) collective-permute-start(bf16[224,512]{1,0:T(8,128)(2,1)S(1)} %get-tuple-element.226), channel_id=1, source_target_pairs={{0,16},{4,20},{8,24},{12,28},{16,0},{20,4},{24,8},{28,12},{1,17},{... | collective-permute-start | bytes 688136 | tf_op jit(solution)/shard_map/ppermute | solution.py:1309
  195.4 14.4 %collective-permute-start.23 = (bf16[320,512]{1,0:T(8,128)(2,1)S(1)}, bf16[320,512]{1,0:T(8,128)(2,1)S(1)}, u32[]{:S(2)}, u32[]{:S(2)}) collective-permute-start(bf16[320,512]{1,0:T(8,128)(2,1)S(1)} %add_convert_fusion.11), channel_id=1, source_target_pairs={{0,2},{1,3},{2,0},{3,1},{4,6},{5,7},{6,4},{7,5},{8,10},{9,11},{10,... | collective-permute-start | bytes 983048 | tf_op jit(solution)/shard_map/ppermute | solution.py:1309
  202.6 11.8 %collective-permute-start.22 = (bf16[160,512]{1,0:T(8,128)(2,1)S(1)}, bf16[160,512]{1,0:T(8,128)(2,1)S(1)}, u32[]{:S(2)}, u32[]{:S(2)}) collective-permute-start(bf16[160,512]{1,0:T(8,128)(2,1)S(1)} %add_convert_fusion.23), channel_id=1, source_target_pairs={{0,1},{1,0},{2,3},{3,2},{4,5},{5,4},{6,7},{7,6},{8,9},{9,8},{10,11... | collective-permute-start | bytes 491528 | tf_op jit(solution)/shard_map/ppermute | solution.py:1309
  210.0 14.4 %collective-permute-start.30 = (bf16[320,512]{1,0:T(8,128)(2,1)S(1)}, bf16[320,512]{1,0:T(8,128)(2,1)S(1)}, u32[]{:S(2)}, u32[]{:S(2)}) collective-permute-start(bf16[320,512]{1,0:T(8,128)(2,1)S(1)} %add_convert_fusion.8), channel_id=1, source_target_pairs={{0,1},{1,0},{2,3},{3,2},{4,5},{5,4},{6,7},{7,6},{8,9},{9,8},{10,11... | collective-permute-start | bytes 983048 | tf_op jit(solution)/shard_map/ppermute | solution.py:1309
  215.4 12.7 %collective-permute-start.26 = (bf16[160,512]{1,0:T(8,128)(2,1)S(1)}, bf16[160,512]{1,0:T(8,128)(2,1)S(1)}, u32[]{:S(2)}, u32[]{:S(2)}) collective-permute-start(bf16[160,512]{1,0:T(8,128)(2,1)S(1)} %add_convert_fusion.22), channel_id=1, source_target_pairs={{0,2},{1,3},{2,0},{3,1},{4,6},{5,7},{6,4},{7,5},{8,10},{9,11},{10,... | collective-permute-start | bytes 491528 | tf_op jit(solution)/shard_map/ppermute | solution.py:1309
  215.6 12.3 %collective-permute-start.29 = (bf16[112,512]{1,0:T(8,128)(2,1)S(1)}, bf16[112,512]{1,0:T(8,128)(2,1)S(1)}, u32[]{:S(2)}, u32[]{:S(2)}) collective-permute-start(bf16[112,512]{1,0:T(8,128)(2,1)S(1)} %pad_maximum_fusion.12), channel_id=1, source_target_pairs={{0,1},{1,0},{2,3},{3,2},{4,5},{5,4},{6,7},{7,6},{8,9},{9,8},{10,11... | collective-permute-start | bytes 344072 | tf_op jit(solution)/shard_map/ppermute | solution.py:1309
  237.1 14.4 %collective-permute-start.39 = (bf16[640,512]{1,0:T(8,128)(2,1)S(1)}, bf16[640,512]{1,0:T(8,128)(2,1)S(1)}, u32[]{:S(2)}, u32[]{:S(2)}) collective-permute-start(bf16[640,512]{1,0:T(8,128)(2,1)S(1)} %pad_maximum_fusion.3), channel_id=1, source_target_pairs={{0,8},{4,12},{8,0},{12,4},{16,24},{20,28},{24,16},{28,20},{1,9},{5... | collective-permute-start | bytes 1966088 | tf_op jit(solution)/shard_map/ppermute | solution.py:1309
  237.1 14.4 %collective-permute-start.40 = (bf16[640,512]{1,0:T(8,128)(2,1)S(1)}, bf16[640,512]{1,0:T(8,128)(2,1)S(1)}, u32[]{:S(2)}, u32[]{:S(2)}) collective-permute-start(bf16[640,512]{1,0:T(8,128)(2,1)S(1)} %pad_maximum_fusion.4), channel_id=1, source_target_pairs={{0,16},{4,20},{8,24},{12,28},{16,0},{20,4},{24,8},{28,12},{1,17},{... | collective-permute-start | bytes 1966088 | tf_op jit(solution)/shard_map/ppermute | solution.py:1309
  252.3 30.6 %collective-permute-start.43 = (bf16[2560,512]{1,0:T(8,128)(2,1)S(1)}, bf16[2560,512]{1,0:T(8,128)(2,1)}, u32[]{:S(2)}, u32[]{:S(2)}) collective-permute-start(bf16[2560,512]{1,0:T(8,128)(2,1)S(1)} %pad_maximum_fusion.refs_4_), channel_id=1, source_target_pairs={{0,4},{4,0},{8,12},{12,8},{16,20},{20,16},{24,28},{28,24},{1,5},{5... | collective-permute-start | bytes 7864328 | tf_op jit(solution)/shard_map/ppermute | solution.py:1309
  258.3 11.8 %collective-permute-start.12 = (bf16[1,144,512]{2,1,0:T(8,128)(2,1)S(1)}, bf16[1,144,512]{2,1,0:T(8,128)(2,1)S(1)}, u32[]{:S(2)}, u32[]{:S(2)}) collective-permute-start(bf16[1,144,512]{2,1,0:T(8,128)(2,1)S(1)} %copy-done.14), channel_id=1, source_target_pairs={{0,2},{1,3},{2,0},{3,1},{4,6},{5,7},{6,4},{7,5},{8,10},{9,11},{10,... | collective-permute-start | bytes 442376 | tf_op jit(solution)/shard_map/ppermute | solution.py:1309
  258.9 18.5 %collective-permute-start.18 = (bf16[512,512]{1,0:T(8,128)(2,1)S(1)}, bf16[512,512]{1,0:T(8,128)(2,1)S(1)}, u32[]{:S(2)}, u32[]{:S(2)}) collective-permute-start(bf16[512,512]{1,0:T(8,128)(2,1)S(1)} %add_convert_fusion.7), channel_id=1, source_target_pairs={{1,2},{2,1},{5,6},{6,5},{9,10},{10,9},{13,14},{14,13},{17,18},{18,... | collective-permute-start | bytes 1572872 | tf_op jit(solution)/shard_map/ppermute | solution.py:1547
  261.5 16.0 %collective-permute-start.19 = (bf16[512,512]{1,0:T(8,128)(2,1)S(1)}, bf16[512,512]{1,0:T(8,128)(2,1)S(1)}, u32[]{:S(2)}, u32[]{:S(2)}) collective-permute-start(bf16[512,512]{1,0:T(8,128)(2,1)S(1)} %add_convert_fusion.6), channel_id=1, source_target_pairs={{0,1},{1,0},{2,3},{3,2},{4,5},{5,4},{6,7},{7,6},{8,9},{9,8},{10,11... | collective-permute-start | bytes 1572872 | tf_op jit(solution)/shard_map/ppermute | solution.py:1548
  269.7 20.8 %collective-permute-start.41 = (bf16[224,512]{1,0:T(8,128)(2,1)S(1)}, bf16[224,512]{1,0:T(8,128)(2,1)}, u32[]{:S(2)}, u32[]{:S(2)}) collective-permute-start(bf16[224,512]{1,0:T(8,128)(2,1)S(1)} %pad_maximum_fusion.10), channel_id=1, source_target_pairs={{0,8},{4,12},{8,0},{12,4},{16,24},{20,28},{24,16},{28,20},{1,9},{5... | collective-permute-start | bytes 688136 | tf_op jit(solution)/shard_map/ppermute | solution.py:1309
  270.1 20.3 %collective-permute-start.42 = (bf16[224,512]{1,0:T(8,128)(2,1)S(1)}, bf16[224,512]{1,0:T(8,128)(2,1)}, u32[]{:S(2)}, u32[]{:S(2)}) collective-permute-start(bf16[224,512]{1,0:T(8,128)(2,1)S(1)} %pad_maximum_fusion.11), channel_id=1, source_target_pairs={{0,16},{4,20},{8,24},{12,28},{16,0},{20,4},{24,8},{28,12},{1,17},{... | collective-permute-start | bytes 688136 | tf_op jit(solution)/shard_map/ppermute | solution.py:1309
  277.4 16.7 %collective-permute-start.45 = (bf16[640,512]{1,0:T(8,128)(2,1)S(1)}, bf16[640,512]{1,0:T(8,128)(2,1)S(1)}, u32[]{:S(2)}, u32[]{:S(2)}) collective-permute-start(bf16[640,512]{1,0:T(8,128)(2,1)S(1)} %pad_maximum_fusion.5.refs_12_), channel_id=1, source_target_pairs={{0,8},{4,12},{8,0},{12,4},{16,24},{20,28},{24,16},{28,20},{1,9},{5... | collective-permute-start | bytes 1966088 | tf_op jit(solution)/shard_map/ppermute | solution.py:1309
  294.4 9.5 %collective-permute-start.46 = (bf16[1280,512]{1,0:T(8,128)(2,1)S(1)}, bf16[1280,512]{1,0:T(8,128)(2,1)S(1)}, u32[]{:S(2)}, u32[]{:S(2)}) collective-permute-start(bf16[1280,512]{1,0:T(8,128)(2,1)S(1)} %pad_maximum_fusion.1.refs_6_.refs_4_), channel_id=1, source_target_pairs={{0,4},{4,0},{8,12},{12,8},{16,20},{20,16},{24,28},{28,24},{1,5},{5... | collective-permute-start | bytes 3932168 | tf_op jit(solution)/shard_map/ppermute | solution.py:1309
  (41 other events, 219.7 us)
